TPU v7x, 32 devices: a whole 2x2x4 slice. The times are simulated.
32 devices in a mesh: region: 2 (over y), curve: 4 (over z), chain: 2 (over x), rep: 2 (over core).
Axes of the slice: x: 2, y: 2, z: 4, core: 2. Of those that a mesh axis runs over, the one named last changes fastest.
Arguments:
- values: bfloat16 [64, 131072], P('chain', ('region', 'curve', 'rep')), parts along dimension 1, may hold values from -6 to 6
- factor: bfloat16 [2048, 64, 320], P(('region', 'curve', 'rep')), parts along dimension 0
- cond: int32 [2048, 4], P(('region', 'curve', 'rep')), parts along dimension 0, may hold values from -1 to 1023, as said below
- live: int32 [16], P(('region', 'curve', 'rep')), parts along dimension 0, may hold values from 64 to 128, as said below
Outputs:
- gradient: float32 [64, 131072], P('chain', ('region', 'curve', 'rep')), parts along dimension 1
There are 2 independent parts, one for each index of `region`. A program takes and returns all parts, laid end to end along the dimension named above; each array names one. Nothing has to cross between parts.
Inputs may be any that keep to these rules, and one draw needn't show every extreme that they name: Slots below a device's count are live blocks, the rest padding; some device has 128 live blocks and another half of 128. `cond`: A row lists distinct live blocks earlier than its own block, each held by the same device along curve+rep or by one of the two devices before it; -1 marks an empty entry, stands after all others in its row, and appears only where fewer than 4 such blocks exist; rows of padding slots are all -1.
All inputs are finite; a program needn't handle non-finite values.
Results may differ from a plain program's by a relative error of at most 0.0023.
Values may be sent and summed in bfloat16 or wider, within the bound.
No kernel may reach another device: no remote copies, remote signals or barrier semaphores. Data moves between devices by JAX's collectives and lax.ppermute only.
A program may use at most 128 MiB of HBM per device.

v0:
```python
import jax
import jax.numpy as jnp
from jax import lax
from jax.sharding import PartitionSpec as P

BS = 64
KN = 4


def from_behind(block, axis, distance):
    devices = range(lax.axis_size(axis))
    route = [(i - distance, i) for i in devices if i - distance in devices]
    return lax.ppermute(block, axis, route)


def body(values, factor, cond, live):
    chains, row_count = values.shape
    blocks = factor.shape[0]
    row_width = factor.shape[2]
    position = lax.axis_index(("curve", "rep"))
    own_blocks = values.reshape(chains, blocks, BS)
    present = cond >= 0
    active = jnp.arange(blocks, dtype=jnp.int32) < live[0]
    window_index = jnp.where(present, cond - (position - 2) * blocks, 0)
    prev_one = from_behind(values, ("curve", "rep"), 1)
    prev_two = from_behind(values, ("curve", "rep"), 2)
    window_rows = jnp.concatenate([prev_two, prev_one, values], axis=1).reshape(
        chains, 3 * blocks, BS
    )
    near_blocks = jnp.take(window_rows, window_index, axis=1)
    near_blocks = jnp.where(present[None, :, :, None], near_blocks, jnp.zeros_like(near_blocks))
    stacked = jnp.concatenate([own_blocks[:, :, None, :], near_blocks], axis=2).reshape(
        chains, blocks, row_width
    )
    residual = jnp.einsum("bij,cbj->cbi", factor, stacked, preferred_element_type=jnp.float32)
    residual = jnp.where(active[None, :, None], residual, jnp.zeros_like(residual)).astype(
        jnp.bfloat16
    )
    terms = jnp.einsum("bij,cbi->cbj", factor, residual, preferred_element_type=jnp.float32)
    gradient = -terms[:, :, :BS]
    back_terms = -terms[:, :, BS:].reshape(chains, blocks, KN, BS)
    back_terms = jnp.where(present[None, :, :, None], back_terms, jnp.zeros_like(back_terms))
    window_terms = (
        jnp.zeros((chains, 3 * blocks, BS), jnp.float32).at[:, window_index].add(back_terms)
    )
    from_one = from_behind(window_terms[:, blocks : 2 * blocks], ("curve", "rep"), -1)
    from_two = from_behind(window_terms[:, :blocks], ("curve", "rep"), -2)
    gradient = gradient + window_terms[:, 2 * blocks :] + from_one + from_two
    return gradient.reshape(chains, row_count)


def solution(mesh):
    placed = (
        P("chain", ("region", "curve", "rep")),
        P(("region", "curve", "rep"), None, None),
        P(("region", "curve", "rep"), None),
        P(("region", "curve", "rep")),
    )
    return jax.shard_map(
        body,
        mesh=mesh,
        in_specs=placed,
        out_specs=P("chain", ("region", "curve", "rep")),
        check_vma=False,
    )
```

profile of v0, /device:TPU:0, one launch (start us, length us, event | category | flops | bytes accessed | tf_op | source)
XLA Modules:
  0.0 210.5 jit_solution(9603542586620499392)
XLA Ops:
  0.0 5.0 %collective-permute-start = (bf16[32,8192]{1,0:T(8,128)(2,1)}, bf16[32,8192]{1,0:T(8,128)(2,1)S(1)}, u32[]{:S(2)}, u32[]{:S(2)}) collective-permute-start(bf16[32,8192]{1,0:T(8,128)(2,1)} %param.4), channel_id=1, source_target_pairs={{0,4},{1,5},{4,8},{5,9},{8,12},{9,13},{2,6},{3,7},{6,10},{7,11},{1... | collective-permute-start | bytes 1572872 | tf_op jit(solution)/shard_map/ppermute | solution.py:13
  5.0 1.5 collective-permute-start.1
  6.5 2.1 broadcast_in_dim_reshape.3
  9.2 0.7 compare_and_fusion
  10.1 1.1 copy.45
  11.2 8.8 %copy.47 = bf16[128,64,320]{2,1,0:T(8,128)(2,1)} copy(bf16[128,64,320]{0,2,1:T(8,128)(2,1)} %param.5) | data formatting | bytes 10485760 | tf_op args[1]
  20.2 4.4 %reshape.21 = bf16[32,384,64]{2,1,0:T(8,128)(2,1)} reshape(bf16[32,24576]{1,0:T(8,128)(2,1)S(1)} %pad_maximum_fusion.1) | data formatting | bytes 3145728 | tf_op jit(solution)/shard_map/reshape | solution.py:27
  24.6 3.9 %copy.43 = bf16[32,384,64]{2,0,1:T(8,128)(2,1)S(1)} copy(bf16[32,384,64]{2,1,0:T(8,128)(2,1)} %reshape.21) | data formatting | bytes 3145728 | tf_op jit(solution)/shard_map/reshape | solution.py:27
  28.5 3.5 %gather_fusion = bf16[512,32,64]{2,1,0:T(8,128)(2,1)} fusion(bf16[32,384,64]{2,0,1:T(8,128)(2,1)S(1)} %copy.43, s32[1024]{0:T(1024)S(1)} %pad_clamp_fusion), kind=kCustom, calls=%fused_computation | custom fusion | bytes 4196352 | tf_op jit(solution)/shard_map/jit(_take)/gather | solution.py:30
  32.1 5.4 %copy.44 = bf16[128,4,32,64]{0,3,1,2:T(8,128)(2,1)S(1)} copy(bf16[128,4,32,64]{3,2,1,0:T(8,128)(2,1)} %bitcast.21) | data formatting | bytes 4194304 | tf_op jit(solution)/shard_map/jit(_take)/gather | solution.py:30
  37.5 0.2 select_bitcast_fusion.1
  37.8 0.8 copy-done
  38.6 1.8 pad_maximum_fusion
  40.3 3.8 %copy.46 = bf16[32,128,320]{2,0,1:T(8,128)(2,1)S(1)} copy(bf16[32,128,320]{1,2,0:T(8,128)(2,1)} %bitcast.23) | data formatting | bytes 5242880 | tf_op jit(solution)/shard_map/reshape | solution.py:32
  44.1 10.6 %fusion.1 = f32[128,32,320]{2,1,0:T(8,128)} fusion(bf16[128,64,320]{2,1,0:T(8,128)(2,1)} %copy.47, bf16[32,128,320]{2,0,1:T(8,128)(2,1)S(1)} %copy.46, pred[128]{0:T(512)(128)(4,1)S(1)} %iota_compare_fusion), kind=kOutput, calls=%fused_computation.9 | convolution fusion | flops 336068608 | bytes 13107328 | tf_op jit(solution)/shard_map/bij,cbi->cbj/dot_general | solution.py:39
  54.8 6.3 %copy.49 = f32[128,32,320]{0,2,1:T(8,128)} copy(f32[128,32,320]{2,1,0:T(8,128)} %fusion.1) | data formatting | bytes 10485760 | tf_op jit(solution)/shard_map/bij,cbi->cbj/dot_general | solution.py:39
  61.1 2.5 %slice_negate_fusion = f32[32,128,256]{1,2,0:T(8,128)S(1)} fusion(f32[32,128,320]{1,2,0:T(8,128)} %bitcast.19), kind=kLoop, calls=%fused_computation.2 | loop fusion | flops 1048576 | bytes 8388608 | tf_op jit(solution)/shard_map/neg | solution.py:41
  63.6 2.4 %select_bitcast_fusion = f32[128,4,32,64]{0,3,1,2:T(8,128)} fusion(f32[32,128,4,64]{1,3,2,0:T(8,128)S(1)} %bitcast.22, pred[128,4]{0,1:T(4,128)(4,1)S(1)} %get-tuple-element.10), kind=kLoop, calls=%fused_computation.3 | loop fusion | flops 1048576 | bytes 8389120 | tf_op jit(solution)/shard_map/jit(_where)/select_n | solution.py:42
  66.0 9.2 %copy.50 = f32[128,4,32,64]{3,2,1,0:T(8,128)} copy(f32[128,4,32,64]{0,3,1,2:T(8,128)} %select_bitcast_fusion) | data formatting | bytes 8388608 | tf_op jit(solution)/shard_map/jit(_where)/select_n | solution.py:42
  75.2 3.5 %broadcast_in_dim.59 = f32[32,384,64]{2,0,1:T(8,128)} broadcast(f32[]{:T(128)} %constant.39.clone.1), dimensions={} | broadcast | bytes 3145732 | tf_op jit(solution)/shard_map/broadcast_in_dim | solution.py:44
  78.7 69.7 %scatter_fusion = f32[32,384,64]{2,0,1:T(8,128)} fusion(f32[32,384,64]{2,0,1:T(8,128)} %broadcast_in_dim.59, s32[512]{0:T(512)S(1)} %reshape.26, f32[512,32,64]{2,1,0:T(8,128)} %bitcast.18), kind=kCustom, calls=%fused_computation.1 | custom fusion | flops 1048576 | bytes 12584960 | tf_op jit(solution)/shard_map/scatter-add | solution.py:44
  148.4 5.5 %fusion.8 = (f32[32,128,64]{2,0,1:T(8,128)S(1)}, f32[32,128,64]{2,0,1:T(8,128)}, f32[32,128,64]{2,0,1:T(8,128)}) fusion(f32[32,384,64]{2,0,1:T(8,128)} %scatter_fusion), kind=kLoop, calls=%fused_computation.22 | loop fusion | bytes 6291456 | tf_op jit(solution)/shard_map/slice | solution.py:48
  153.9 3.6 %copy.53 = f32[32,128,64]{1,2,0:T(8,128)} copy(f32[32,128,64]{2,0,1:T(8,128)} %get-tuple-element.8) | data formatting | bytes 2097152 | tf_op jit(solution)/shard_map/slice | solution.py:47
  157.5 3.7 %copy.52 = f32[32,128,64]{1,2,0:T(8,128)} copy(f32[32,128,64]{2,0,1:T(8,128)} %get-tuple-element.9) | data formatting | bytes 2097152 | tf_op jit(solution)/shard_map/slice | solution.py:46
  161.2 1.3 collective-permute-start.2
  162.5 1.3 collective-permute-start.3
  163.8 1.3 copy.55
  165.0 2.1 collective-permute-done.2
  167.1 36.7 %collective-permute-done.3 = f32[32,128,64]{1,2,0:T(8,128)} collective-permute-done((f32[32,128,64]{1,2,0:T(8,128)}, f32[32,128,64]{1,2,0:T(8,128)}, u32[]{:S(2)}, u32[]{:S(2)}) %collective-permute-start.3) | collective-permute-done | bytes 1048608 | tf_op jit(solution)/shard_map/ppermute | solution.py:13
  203.8 3.2 %fusion.4 = f32[32,128,64]{1,2,0:T(8,128)} fusion(f32[32,128,64]{1,2,0:T(8,128)} %collective-permute-done.3, f32[32,128,64]{1,2,0:T(8,128)} %collective-permute-done.2, f32[32,128,64]{1,2,0:T(8,128)S(1)} %copy.55, f32[32,128,320]{1,2,0:T(8,128)} %bitcast.20), kind=kLoop, calls=%fused_computation.13 | loop fusion | flops 1048576 | bytes 5242880 | tf_op jit(solution)/shard_map/add | solution.py:48
  207.1 1.8 copy.54
  208.9 1.6 reshape.23
  (10 shorter events, 0.3 us)
Async XLA Ops:
  0.0 20.0 %collective-permute-start = (bf16[32,8192]{1,0:T(8,128)(2,1)}, bf16[32,8192]{1,0:T(8,128)(2,1)S(1)}, u32[]{:S(2)}, u32[]{:S(2)}) collective-permute-start(bf16[32,8192]{1,0:T(8,128)(2,1)} %param.4), channel_id=1, source_target_pairs={{0,4},{1,5},{4,8},{5,9},{8,12},{9,13},{2,6},{3,7},{6,10},{7,11},{1... | collective-permute-start | bytes 1572872 | tf_op jit(solution)/shard_map/ppermute | solution.py:13
  5.0 15.1 %collective-permute-start.1 = (bf16[32,8192]{1,0:T(8,128)(2,1)}, bf16[32,8192]{1,0:T(8,128)(2,1)S(1)}, u32[]{:S(2)}, u32[]{:S(2)}) collective-permute-start(bf16[32,8192]{1,0:T(8,128)(2,1)} %param.4), channel_id=1, source_target_pairs={{0,1},{1,4},{4,5},{5,8},{8,9},{9,12},{12,13},{2,3},{3,6},{6,7},{7,... | collective-permute-start | bytes 1572872 | tf_op jit(solution)/shard_map/ppermute | solution.py:13
  11.2 8.8 %copy-start.1 = (bf16[32,8192]{1,0:T(8,128)(2,1)S(1)}, bf16[32,8192]{1,0:T(8,128)(2,1)}, u32[]{:S(2)}) copy-start(bf16[32,8192]{1,0:T(8,128)(2,1)} %param.4) | copy-start | bytes 1572868
  37.5 1.0 copy-start
  161.2 6.0 %collective-permute-start.2 = (f32[32,128,64]{1,2,0:T(8,128)}, f32[32,128,64]{1,2,0:T(8,128)}, u32[]{:S(2)}, u32[]{:S(2)}) collective-permute-start(f32[32,128,64]{1,2,0:T(8,128)} %copy.52), channel_id=1, source_target_pairs={{1,0},{4,1},{5,4},{8,5},{9,8},{12,9},{13,12},{3,2},{6,3},{7,6},{10... | collective-permute-start | bytes 3145736 | tf_op jit(solution)/shard_map/ppermute | solution.py:13
  162.5 41.4 %collective-permute-start.3 = (f32[32,128,64]{1,2,0:T(8,128)}, f32[32,128,64]{1,2,0:T(8,128)}, u32[]{:S(2)}, u32[]{:S(2)}) collective-permute-start(f32[32,128,64]{1,2,0:T(8,128)} %copy.53), channel_id=1, source_target_pairs={{4,0},{5,1},{8,4},{9,5},{12,8},{13,9},{6,2},{7,3},{10,6},{11,7},{1... | collective-permute-start | bytes 3145736 | tf_op jit(solution)/shard_map/ppermute | solution.py:13
where the time goes:
time: 211 us
  other arithmetic  80.6 us (38%)
  local copies, waits for them, and re-layouts  70.7 us (34%)
  waiting for transfers between devices  38.8 us (18%)
  matrix products  10.6 us (5%)
  starting transfers between devices  9.02 us (4%)
    scatter-add x1, other arithmetic, body(): jnp.zeros((chains, 3 * blocks, BS), jnp.float32).at[:, window_index]  69.7 us
    ppermute x4, waiting for transfers between devices, from_behind(): return lax.ppermute(block, axis, route)  38.8 us
    unnamed x6, local copies, waits for them, and re-layouts  10.9 us
    dot_general x1, matrix products, body(): jnp.einsum('bij,cbi->cbj', factor, residual, preferred_element_type=jnp.f...  10.6 us
    select_n x1, local copies, waits for them, and re-layouts, body(): jnp.where(present[None, :, :, None], back_terms, jnp.zeros_like(back_terms))  9.23 us
    ppermute x4, starting transfers between devices, from_behind(): return lax.ppermute(block, axis, route)  9.02 us
    gather x2, local copies, waits for them, and re-layouts, body(): near_blocks = jnp.take(window_rows, window_index, axis=1)  8.98 us
    reshape x2, local copies, waits for them, and re-layouts, body(): jnp.concatenate([prev_two, prev_one, values], axis=1)  8.33 us
  transfers between devices with their start and end apart: 4, of which 2 were waited for; matrix products, arithmetic and copies ran while one was open for 7% of the time, Pallas kernels for 0%

commit v1 on v0

v1 whole, which is shorter than its diff:
```python
import functools

import jax
import jax.numpy as jnp
from jax import lax
from jax.experimental import pallas as pl
from jax.experimental.pallas import tpu as pltpu
from jax.sharding import PartitionSpec as P

BS = 64
KN = 4
LANES = 128
GROUP = 4
PIECES = 8
CHUNKS = 1


def shift(block, axis, distance):
    size = lax.axis_size(axis)
    return lax.ppermute(
        block, axis, [(i - distance, i) for i in range(size) if 0 <= i - distance < size]
    )


def swap(block):
    return lax.ppermute(block, "rep", [(0, 1), (1, 0)])


def half_roll(tile):
    return jnp.concatenate([tile[..., BS:], tile[..., :BS]], axis=-1)


def kernel(
    first_row, index, live, two, one, own, factor,
    out_two, out_one, out_own,
    held, window, low, high, sems,
):
    chains = two.shape[0]
    blocks = held.shape[0]
    tiles = blocks // 2
    per_piece = blocks // PIECES
    copies = [
        pltpu.make_async_copy(
            factor.at[pl.ds(i * per_piece, per_piece)],
            held.at[pl.ds(i * per_piece, per_piece)],
            sems.at[i],
        )
        for i in range(PIECES)
    ]
    for copy in copies:
        copy.start()

    rows = pl.ds(first_row, chains)
    for region, source in enumerate((two, one, own)):
        source_rows = rows if region == 2 else slice(None)

        def spread(t, carry, region=region, source=source, source_rows=source_rows):
            tile = source[source_rows, pl.ds(pl.multiple_of(t * LANES, LANES), LANES)]
            window[region * blocks + 2 * t] = tile
            window[region * blocks + 2 * t + 1] = half_roll(tile)
            return carry

        lax.fori_loop(0, tiles, spread, 0, unroll=8)
    window[pl.ds(3 * blocks, 2)] = jnp.zeros((2, chains, LANES), window.dtype)

    def clear(i, carry):
        zero = jnp.zeros((8, chains, LANES), jnp.float32)
        low[pl.ds(i * 8, 8)] = zero
        high[pl.ds(i * 8, 8)] = zero
        return carry

    lax.fori_loop(0, 2 * blocks // 8, clear, 0, unroll=2)
    low[pl.ds(3 * blocks, 1)] = jnp.zeros((1, chains, LANES), jnp.float32)
    high[pl.ds(3 * blocks, 1)] = jnp.zeros((1, chains, LANES), jnp.float32)

    in_low = lax.broadcasted_iota(jnp.int32, (chains, LANES), 1) < BS
    shape = (GROUP * chains, GROUP * BS)
    row_block = lax.broadcasted_iota(jnp.int32, shape, 0) // chains
    lane_block = lax.broadcasted_iota(jnp.int32, shape, 1) // BS
    diagonal = row_block == lane_block
    live_count = live[0]

    def group(q, carry):
        first = q * GROUP
        stacked = []
        places = []
        for b in range(GROUP):
            g = first + b
            at = [index[g * KN + k] for k in range(KN)]
            places.append(at)
            stacked.append(
                jnp.concatenate(
                    [
                        jnp.where(in_low, window[2 * blocks + g], window[at[0] ^ 1]),
                        jnp.where(in_low, window[at[1]], window[at[2] ^ 1]),
                        window[at[3]][:, :BS],
                    ],
                    axis=1,
                )
            )
        stacked = jnp.concatenate(stacked, axis=0)
        maps = held[pl.ds(first, GROUP)].reshape(GROUP * BS, BS * (KN + 1))
        residual = lax.dot_general(
            stacked, maps, (((1,), (1,)), ((), ())), preferred_element_type=jnp.float32
        )
        kept = diagonal & (lane_block < live_count - first)
        residual = jnp.where(kept, residual, 0.0).astype(jnp.bfloat16)
        terms = jnp.dot(residual, maps, preferred_element_type=jnp.float32)
        for b in range(GROUP):
            g = first + b
            at = places[b]
            t0 = terms[b * chains : (b + 1) * chains, :LANES]
            t1 = terms[b * chains : (b + 1) * chains, LANES : 2 * LANES]
            t2 = terms[b * chains : (b + 1) * chains, 2 * LANES :]
            t2 = jnp.concatenate([t2, t2], axis=1)
            u0, l1, u2, l3 = high[at[0]], low[at[1]], high[at[2]], low[at[3]]
            high[at[0]] = u0 + t0
            low[at[1]] = l1 + t1
            high[at[2]] = u2 + t1
            low[at[3]] = l3 + t2
            low[2 * blocks + g] = t0
            high[2 * blocks + g] = jnp.zeros_like(t0)
        return carry

    for i, copy in enumerate(copies):
        copy.wait()
        lax.fori_loop(i * per_piece // GROUP, (i + 1) * per_piece // GROUP, group, 0)

    for region, target in enumerate((out_two, out_one, out_own)):

        def gather(t, carry, region=region, target=target):
            even = region * blocks + 2 * t
            straight = jnp.where(in_low, low[even], high[even + 1])
            crossed = jnp.where(in_low, low[even + 1], high[even])
            total = -(straight + half_roll(crossed))
            target[:, pl.ds(pl.multiple_of(t * LANES, LANES), LANES)] = total.astype(target.dtype)
            return carry

        lax.fori_loop(0, tiles, gather, 0, unroll=8)


def local_terms(first_row, index, live, two, one, own, factor):
    chains, row_count = two.shape
    blocks = factor.shape[0]
    width = factor.shape[2]
    vmem = pl.BlockSpec(memory_space=pltpu.VMEM)
    smem = pl.BlockSpec(memory_space=pltpu.SMEM)
    slots = 3 * blocks + 2
    return pl.pallas_call(
        functools.partial(kernel, first_row),
        out_shape=(
            jax.ShapeDtypeStruct((chains, row_count), jnp.bfloat16),
            jax.ShapeDtypeStruct((chains, row_count), jnp.float32),
            jax.ShapeDtypeStruct((chains, row_count), jnp.float32),
        ),
        in_specs=[smem, smem, vmem, vmem, vmem, pl.BlockSpec(memory_space=pl.ANY)],
        out_specs=(vmem, vmem, vmem),
        scratch_shapes=[
            pltpu.VMEM((blocks, BS, width), jnp.bfloat16),
            pltpu.VMEM((slots, chains, LANES), jnp.bfloat16),
            pltpu.VMEM((slots, chains, LANES), jnp.float32),
            pltpu.VMEM((slots, chains, LANES), jnp.float32),
            pltpu.SemaphoreType.DMA((PIECES,)),
        ],
        compiler_params=pltpu.CompilerParams(vmem_limit_bytes=44 * 2**20),
        cost_estimate=pl.CostEstimate(
            flops=16 * blocks * BS * width * chains, bytes_accessed=8 * 2**20, transcendentals=0
        ),
    )(index, live, two, one, own, factor)


def body(values, factor, cond, live):
    chains, row_count = values.shape
    blocks = factor.shape[0]
    position = lax.axis_index(("curve", "rep"))
    core = lax.axis_index("rep")
    index = jnp.where(cond >= 0, cond - (position - 2) * blocks, 3 * blocks).reshape(-1)
    part = chains // CHUNKS
    arrived = [
        shift(values[c * part : (c + 1) * part], "curve", 1) for c in range(CHUNKS)
    ]
    results = []
    for c in range(CHUNKS):
        own = values[c * part : (c + 1) * part]
        one = swap(jnp.where(core == 0, own, arrived[c]))
        to_two, to_one, mine = local_terms(c * part, index, live, arrived[c], one, values, factor)
        across = swap(to_one)
        to_two = to_two.astype(jnp.float32) + jnp.where(core == 1, across, jnp.zeros_like(across))
        back = shift(to_two.astype(jnp.bfloat16), "curve", -1)
        results.append(
            mine + jnp.where(core == 0, across, jnp.zeros_like(across)) + back.astype(jnp.float32)
        )
    return jnp.concatenate(results, axis=0)


def solution(mesh):
    placed = (
        P("chain", ("region", "curve", "rep")),
        P(("region", "curve", "rep"), None, None),
        P(("region", "curve", "rep"), None),
        P(("region", "curve", "rep")),
    )
    return jax.shard_map(
        body,
        mesh=mesh,
        in_specs=placed,
        out_specs=P("chain", ("region", "curve", "rep")),
        check_vma=False,
    )
```

time: 211 us -> 71.4 us (0.34)
  the two profiles are of different devices: /device:TPU:0 before, /device:TPU:1 now
where the time goes in v1:
time: 71.4 us; the launch traced here: 70.3 us
  waiting for transfers between devices  28.5 us (40%)
  Pallas kernels  22 us (31%)
  local copies, waits for them, and re-layouts  8.97 us (13%)
  starting transfers between devices  8.1 us (11%)
  other arithmetic  2 us (3%)
    ppermute x2, waiting for transfers between devices, shift(): lax.ppermute(block, axis, [(i - distance, i) for i in range(size) if 0 <=...  25.7 us
    pallas_call x1, Pallas kernels, local_terms(): pl.pallas_call(functools.partial(kernel, first_row), out_shape=(jax.Shape...  22 us
    unnamed x3, local copies, waits for them, and re-layouts  8.75 us
    ppermute x2, starting transfers between devices, shift(): lax.ppermute(block, axis, [(i - distance, i) for i in range(size) if 0 <=...  5.34 us
    ppermute x2, waiting for transfers between devices, swap(): return lax.ppermute(block, 'rep', [(0, 1), (1, 0)])  2.83 us
    ppermute x2, starting transfers between devices, swap(): return lax.ppermute(block, 'rep', [(0, 1), (1, 0)])  2.76 us
  transfers between devices with their start and end apart: 4, of which 3 were waited for; matrix products, arithmetic and copies ran while one was open for 14% of the time, Pallas kernels for 0%

profile of v1, /device:TPU:1, one launch (start us, length us, event | category | flops | bytes accessed | tf_op | source)
XLA Modules:
  0.0 70.3 jit_solution(3185711108935832929)
XLA Ops:
  0.0 4.0 %collective-permute-start = (bf16[32,8192]{1,0:T(8,128)(2,1)}, bf16[32,8192]{1,0:T(8,128)(2,1)S(1)}, u32[]{:S(2)}, u32[]{:S(2)}) collective-permute-start(bf16[32,8192]{1,0:T(8,128)(2,1)} %own.1), channel_id=1, source_target_pairs={{0,4},{4,8},{8,12},{1,5},{5,9},{9,13},{2,6},{6,10},{10,14},{3,7},{... | collective-permute-start | bytes 1572872 | tf_op jit(solution)/shard_map/ppermute | solution.py:20
  4.1 0.0 copy-start
  4.1 10.8 %collective-permute-done.two = bf16[32,8192]{1,0:T(8,128)(2,1)S(1)} collective-permute-done((bf16[32,8192]{1,0:T(8,128)(2,1)}, bf16[32,8192]{1,0:T(8,128)(2,1)S(1)}, u32[]{:S(2)}, u32[]{:S(2)}) %collective-permute-start) | collective-permute-done | bytes 524320 | tf_op jit(solution)/shard_map/ppermute | solution.py:20
  14.9 0.1 broadcast_select_fusion
  15.0 2.6 %collective-permute-start.1 = (bf16[32,8192]{1,0:T(8,128)(2,1)S(1)}, bf16[32,8192]{1,0:T(8,128)(2,1)S(1)}, u32[]{:S(2)}, u32[]{:S(2)}) collective-permute-start(bf16[32,8192]{1,0:T(8,128)(2,1)S(1)} %broadcast_select_fusion), channel_id=1, source_target_pairs={{0,1},{1,0},{2,3},{3,2},{4,5},{5,4},{6,7},{7,6},{8,9},{9,8},{10,11... | collective-permute-start | bytes 1572872 | tf_op jit(solution)/shard_map/ppermute | solution.py:26
  18.3 0.7 subtract_select_fusion
  19.0 0.1 copy.6
  19.1 0.1 reshape.3.index
  19.2 8.7 %copy.7.factor = bf16[128,64,320]{2,1,0:T(8,128)(2,1)} copy(bf16[128,64,320]{0,2,1:T(8,128)(2,1)} %param.5) | data formatting | bytes 10485760 | tf_op args[1]
  27.9 0.0 collective-permute-done.1.one
  27.9 0.0 copy-done
  27.9 22.0 %shard_map.46 = (bf16[32,8192]{1,0:T(8,128)(2,1)S(1)}, f32[32,8192]{1,0:T(8,128)}, f32[32,8192]{1,0:T(8,128)S(1)}) custom-call(s32[512]{0:T(512)S(1)} %reshape.3.index, s32[1]{0:T(128)S(6)} %copy.8.live, bf16[32,8192]{1,0:T(8,128)(2,1)S(1)} %collective-permute-done.two, bf16[32,8192]{1,0:T(8,128)(2,1)S(1)} %collective-permute-done.1.one, ...), custom_call_target="tpu_custom_call" | custom-call | flops 1342177280 | bytes 8388608 | tf_op jit(solution)/shard_map/pallas_call | solution.py:149
  50.0 0.1 collective-permute-start.2
  50.1 2.8 %collective-permute-done.2 = f32[32,8192]{1,0:T(8,128)S(1)} collective-permute-done((f32[32,8192]{1,0:T(8,128)}, f32[32,8192]{1,0:T(8,128)S(1)}, u32[]{:S(2)}, u32[]{:S(2)}) %collective-permute-start.2) | collective-permute-done | bytes 1048608 | tf_op jit(solution)/shard_map/ppermute | solution.py:26
  52.9 0.1 add_convert_fusion
  53.0 1.3 %collective-permute-start.3 = (bf16[32,8192]{1,0:T(8,128)(2,1)S(1)}, bf16[32,8192]{1,0:T(8,128)(2,1)S(1)}, u32[]{:S(2)}, u32[]{:S(2)}) collective-permute-start(bf16[32,8192]{1,0:T(8,128)(2,1)S(1)} %add_convert_fusion), channel_id=1, source_target_pairs={{4,0},{8,4},{12,8},{5,1},{9,5},{13,9},{6,2},{10,6},{14,10},{7,3},{... | collective-permute-start | bytes 1572872 | tf_op jit(solution)/shard_map/ppermute | solution.py:20
  54.3 14.9 %collective-permute-done.3 = bf16[32,8192]{1,0:T(8,128)(2,1)S(1)} collective-permute-done((bf16[32,8192]{1,0:T(8,128)(2,1)S(1)}, bf16[32,8192]{1,0:T(8,128)(2,1)S(1)}, u32[]{:S(2)}, u32[]{:S(2)}) %collective-permute-start.3) | collective-permute-done | bytes 524320 | tf_op jit(solution)/shard_map/ppermute | solution.py:20
  69.2 1.1 %convert_add_fusion = f32[32,8192]{1,0:T(8,128)} fusion(bf16[32,8192]{1,0:T(8,128)(2,1)S(1)} %collective-permute-done.3, f32[32,8192]{1,0:T(8,128)S(1)} %get-tuple-element.8, f32[32,8192]{1,0:T(8,128)S(1)} %collective-permute-done.2, pred[]{:T(512)S(6)} %eq.7), kind=kLoop, calls=%fused_computation | loop fusion | flops 1048576 | bytes 3670017 | tf_op jit(solution)/shard_map/add | solution.py:191
Async XLA Ops:
  0.0 14.9 %collective-permute-start = (bf16[32,8192]{1,0:T(8,128)(2,1)}, bf16[32,8192]{1,0:T(8,128)(2,1)S(1)}, u32[]{:S(2)}, u32[]{:S(2)}) collective-permute-start(bf16[32,8192]{1,0:T(8,128)(2,1)} %own.1), channel_id=1, source_target_pairs={{0,4},{4,8},{8,12},{1,5},{5,9},{9,13},{2,6},{6,10},{10,14},{3,7},{... | collective-permute-start | bytes 1572872 | tf_op jit(solution)/shard_map/ppermute | solution.py:20
  4.1 23.9 %copy-start = (bf16[32,8192]{1,0:T(8,128)(2,1)S(1)}, bf16[32,8192]{1,0:T(8,128)(2,1)}, u32[]{:S(2)}) copy-start(bf16[32,8192]{1,0:T(8,128)(2,1)} %own.1) | copy-start | bytes 1572868
  15.0 13.0 %collective-permute-start.1 = (bf16[32,8192]{1,0:T(8,128)(2,1)S(1)}, bf16[32,8192]{1,0:T(8,128)(2,1)S(1)}, u32[]{:S(2)}, u32[]{:S(2)}) collective-permute-start(bf16[32,8192]{1,0:T(8,128)(2,1)S(1)} %broadcast_select_fusion), channel_id=1, source_target_pairs={{0,1},{1,0},{2,3},{3,2},{4,5},{5,4},{6,7},{7,6},{8,9},{9,8},{10,11... | collective-permute-start | bytes 1572872 | tf_op jit(solution)/shard_map/ppermute | solution.py:26
  50.0 2.9 %collective-permute-start.2 = (f32[32,8192]{1,0:T(8,128)}, f32[32,8192]{1,0:T(8,128)S(1)}, u32[]{:S(2)}, u32[]{:S(2)}) collective-permute-start(f32[32,8192]{1,0:T(8,128)} %get-tuple-element.9), channel_id=1, source_target_pairs={{0,1},{1,0},{2,3},{3,2},{4,5},{5,4},{6,7},{7,6},{8,9},{9,8},{10,11... | collective-permute-start | bytes 3145736 | tf_op jit(solution)/shard_map/ppermute | solution.py:26
  53.0 16.2 %collective-permute-start.3 = (bf16[32,8192]{1,0:T(8,128)(2,1)S(1)}, bf16[32,8192]{1,0:T(8,128)(2,1)S(1)}, u32[]{:S(2)}, u32[]{:S(2)}) collective-permute-start(bf16[32,8192]{1,0:T(8,128)(2,1)S(1)} %add_convert_fusion), channel_id=1, source_target_pairs={{4,0},{8,4},{12,8},{5,1},{9,5},{13,9},{6,2},{10,6},{14,10},{7,3},{... | collective-permute-start | bytes 1572872 | tf_op jit(solution)/shard_map/ppermute | solution.py:20

commit v2 on v0

v2 whole, which is shorter than its diff:
```python
import jax
import jax.numpy as jnp
from jax import lax
from jax.experimental import pallas as pl
from jax.experimental.pallas import tpu as pltpu
from jax.sharding import PartitionSpec as P

BS = 64
KN = 4
LANES = 128
GROUP = 4
UNROLL = 16
PIECES = 4

VMEM = pl.BlockSpec(memory_space=pltpu.VMEM)
SMEM = pl.BlockSpec(memory_space=pltpu.SMEM)
HBM = pl.BlockSpec(memory_space=pltpu.HBM)


def to_next_chip(block, core):
    size = lax.axis_size("curve")
    return lax.ppermute(
        block, ("curve", "rep"), [(2 * z + core, 2 * z + 2 + core) for z in range(size - 1)]
    )


def from_next_chip(block, core):
    size = lax.axis_size("curve")
    return lax.ppermute(
        block, ("curve", "rep"), [(2 * z + 2 + core, 2 * z + core) for z in range(size - 1)]
    )


def swap(block):
    return lax.ppermute(block, "rep", [(0, 1), (1, 0)])


def half_roll(tile):
    return pltpu.roll(tile, BS, tile.ndim - 1)


def lane_tile(t):
    return pl.ds(pl.multiple_of(t * LANES, LANES), LANES)


def low_lanes(rows):
    return lax.broadcasted_iota(jnp.int32, (rows, LANES), 1) < BS


def cross(low, first, second):
    kept = jnp.where(low, first, second)
    moved = half_roll(jnp.where(low, second, first))
    return jnp.where(low, kept, moved), jnp.where(low, moved, kept)


def spread(source, window, first_block):
    def step(t, carry):
        tile = source[:, lane_tile(t)]
        window[first_block + 2 * t] = tile
        window[first_block + 2 * t + 1] = half_roll(tile.astype(jnp.float32)).astype(tile.dtype)
        return carry

    lax.fori_loop(0, source.shape[1] // LANES, step, 0, unroll=8)


def collect(total, first_block, target):
    low = low_lanes(total.shape[1])

    def step(t, carry):
        even = first_block + 2 * t
        upper, lower = cross(low, total[even], total[even + 1])
        tile = jnp.concatenate([upper, lower], axis=0).astype(target.dtype)
        target[:, lane_tile(t)] = tile
        return carry

    lax.fori_loop(0, target.shape[1] // LANES, step, 0, unroll=8)


def turn_kernel(flipped, factor, staged, sems):
    pieces = staged.shape[0]
    rows = staged.shape[1]
    copies = [
        pltpu.make_async_copy(flipped.at[pl.ds(i * rows, rows)], staged.at[i], sems.at[i])
        for i in range(pieces)
    ]
    for copy in copies:
        copy.start()
    for i, copy in enumerate(copies):
        copy.wait()
        factor[:, pl.ds(i * rows, rows), :] = jnp.transpose(staged[i], (2, 0, 1))


def payload_kernel(core, own, arrived, factor, index, target):
    @pl.when(core[0] == 0)
    def _():
        target[...] = own[...]

    @pl.when(core[0] != 0)
    def _():
        target[...] = arrived[...]


def own_kernel(own, index, window, total, again):
    again[...] = own[...]
    blocks = own.shape[1] // BS
    half = total.shape[1]
    spread(own, window, 2 * blocks)
    window[pl.ds(3 * blocks, 2)] = jnp.zeros((2,) + window.shape[1:], window.dtype)

    def clear(i, carry):
        total[pl.ds(i * 8, 8)] = jnp.zeros((8, half, LANES), jnp.float32)
        return carry

    lax.fori_loop(0, 2 * blocks // 8, clear, 0, unroll=4)
    total[3 * blocks] = jnp.zeros((half, LANES), jnp.float32)


def halo_kernel(core, one, two_even, two_odd, window_in, window):
    spread(one, window, one.shape[1] // BS)

    @pl.when(core[0] == 0)
    def _():
        spread(two_even, window, 0)

    @pl.when(core[0] != 0)
    def _():
        spread(two_odd, window, 0)


def main_kernel(
    index, live, window, total_in, factor, out_one, total, residuals,
):
    chains = window.shape[1]
    half = chains // 2
    blocks = factor.shape[0]

    low = low_lanes(chains)
    half_low = low_lanes(half)
    shape = (GROUP * chains, GROUP * BS)
    row_block = lax.broadcasted_iota(jnp.int32, shape, 0) // chains
    lane_block = lax.broadcasted_iota(jnp.int32, shape, 1) // BS
    diagonal = row_block == lane_block
    live_count = live[0]

    def pull(q, carry):
        first = q * GROUP
        stacked = []
        for b in range(GROUP):
            g = first + b
            at = [index[g * KN + k] for k in range(KN)]
            stacked.append(
                jnp.concatenate(
                    [
                        jnp.where(low, window[2 * blocks + g], window[at[0] ^ 1]),
                        jnp.where(low, window[at[1]], window[at[2] ^ 1]),
                        window[at[3]][:, :BS],
                    ],
                    axis=1,
                )
            )
        stacked = jnp.concatenate(stacked, axis=0)
        maps = factor[pl.ds(first, GROUP)].reshape(GROUP * BS, BS * (KN + 1))
        residual = lax.dot_general(
            stacked, maps, (((1,), (1,)), ((), ())), preferred_element_type=jnp.float32
        )
        kept = diagonal & (lane_block < live_count - first)
        residuals[q] = jnp.where(kept, -residual, 0.0).astype(jnp.bfloat16)
        return carry

    def push(q, carry):
        first = q * GROUP
        maps = factor[pl.ds(first, GROUP)].reshape(GROUP * BS, BS * (KN + 1))
        terms = jnp.dot(residuals[q], maps, preferred_element_type=jnp.float32)
        for b in range(GROUP):
            g = first + b
            at = [index[g * KN + k] for k in range(KN)]
            a = terms[b * chains : b * chains + half]
            z = terms[b * chains + half : (b + 1) * chains]
            mine, t0 = cross(half_low, a[:, :LANES], z[:, :LANES])
            t1, t2 = cross(half_low, a[:, LANES : 2 * LANES], z[:, LANES : 2 * LANES])
            t3 = jnp.concatenate([a[:, 2 * LANES :], z[:, 2 * LANES :]], axis=1)
            old = [total[at[k]] for k in range(KN)]
            for k, term in enumerate((t0, t1, t2, t3)):
                total[at[k]] = old[k] + term
            total[2 * blocks + g] = mine
        return carry

    lax.fori_loop(0, blocks // GROUP, pull, 0, unroll=UNROLL)
    lax.fori_loop(0, blocks // GROUP, push, 0, unroll=UNROLL)
    collect(total, blocks, out_one)


def add_across(core, keeper, total, across, target, first_block):
    low = low_lanes(total.shape[1])
    share = jnp.where(core[0] == keeper, 1.0, 0.0)

    def step(t, carry):
        even = first_block + 2 * t
        upper, lower = cross(low, total[even], total[even + 1])
        tile = jnp.concatenate([upper, lower], axis=0) + share * across[:, lane_tile(t)]
        target[:, lane_tile(t)] = tile.astype(target.dtype)
        return carry

    lax.fori_loop(0, target.shape[1] // LANES, step, 0, unroll=8)


def two_kernel(total, target):
    collect(total, 0, target)


def joint_kernel(core, total, across, target):
    add_across(core, 1, total, across, target, 0)


def mine_kernel(core, total, across, target):
    add_across(core, 0, total, across, target, 2 * (target.shape[1] // BS))


def call(kernel, outs, specs, args, out_specs=VMEM, **more):
    return pl.pallas_call(
        kernel,
        out_shape=outs,
        in_specs=specs,
        out_specs=out_specs,
        **more,
    )(*args)


LITTLE = pl.CostEstimate(flops=0, bytes_accessed=1024, transcendentals=0)


def params(mib):
    return pltpu.CompilerParams(vmem_limit_bytes=mib * 2**20)


def body(values, factor, cond, live):
    chains, row_count = values.shape
    blocks, rows, width = factor.shape
    slots = 3 * blocks + 2
    position = lax.axis_index(("curve", "rep"))
    core = lax.axis_index("rep").reshape(1)
    index = jnp.where(cond >= 0, cond - (position - 2) * blocks, 3 * blocks).reshape(-1)
    narrow = jax.ShapeDtypeStruct((chains, row_count), jnp.bfloat16)
    wide = jax.ShapeDtypeStruct((chains, row_count), jnp.float32)
    window_shape = jax.ShapeDtypeStruct((slots, chains, LANES), jnp.bfloat16)
    total_shape = jax.ShapeDtypeStruct((slots, chains // 2, LANES), jnp.float32)

    two_odd = to_next_chip(values, 1)
    window, total, again = call(
        own_kernel,
        (window_shape, total_shape, narrow),
        [VMEM, SMEM],
        (values, index),
        out_specs=(VMEM, VMEM, VMEM),
        compiler_params=params(4),
        cost_estimate=LITTLE,
    )
    two_even = to_next_chip(again, 0)
    factor = call(
        turn_kernel,
        jax.ShapeDtypeStruct(factor.shape, factor.dtype),
        [HBM],
        (jnp.transpose(factor, (1, 2, 0)),),
        scratch_shapes=[
            pltpu.VMEM((PIECES, rows // PIECES, width, blocks), factor.dtype),
            pltpu.SemaphoreType.DMA((PIECES,)),
        ],
        compiler_params=params(16),
        cost_estimate=pl.CostEstimate(flops=0, bytes_accessed=14 * 2**20, transcendentals=0),
    )
    payload = call(
        payload_kernel,
        narrow,
        [SMEM, VMEM, VMEM, VMEM, SMEM],
        (core, values, two_odd, factor, index),
        compiler_params=params(4), cost_estimate=LITTLE,
    )
    one = swap(payload)
    window = call(
        halo_kernel,
        window_shape,
        [SMEM, VMEM, VMEM, VMEM, VMEM],
        (core, one, two_even, two_odd, window),
        input_output_aliases={4: 0}, compiler_params=params(4), cost_estimate=LITTLE
    )
    to_one, total = call(
        main_kernel,
        (wide, total_shape),
        [SMEM, SMEM, VMEM, VMEM, VMEM],
        (index, live, window, total, factor),
        out_specs=(VMEM, VMEM),
        scratch_shapes=[
            pltpu.VMEM((blocks // GROUP, GROUP * chains, GROUP * BS), jnp.bfloat16),
        ],
        input_output_aliases={3: 1},
        compiler_params=params(12),
        cost_estimate=pl.CostEstimate(
            flops=16 * blocks * rows * width * chains,
            bytes_accessed=8 * 2**20,
            transcendentals=0,
        ),
    )
    across = swap(to_one)
    to_two = call(two_kernel, narrow, [VMEM], (total,), compiler_params=params(4), cost_estimate=LITTLE)
    back = from_next_chip(to_two, 0)
    joint = call(joint_kernel, narrow, [SMEM, VMEM, VMEM], (core, total, across), compiler_params=params(4), cost_estimate=LITTLE)
    joint = from_next_chip(joint, 1)
    mine = call(mine_kernel, wide, [SMEM, VMEM, VMEM], (core, total, across), compiler_params=params(4), cost_estimate=LITTLE)
    return mine + jnp.where(core == 0, back, joint).astype(jnp.float32)


def solution(mesh):
    placed = (
        P("chain", ("region", "curve", "rep")),
        P(("region", "curve", "rep"), None, None),
        P(("region", "curve", "rep"), None),
        P(("region", "curve", "rep")),
    )
    return jax.shard_map(
        body,
        mesh=mesh,
        in_specs=placed,
        out_specs=P("chain", ("region", "curve", "rep")),
        check_vma=False,
    )
```

time: 211 us -> 43.3 us (0.21)
  the two profiles are of different devices: /device:TPU:0 before, /device:TPU:1 now
where the time goes in v2:
time: 43.3 us; the launch traced here: 43 us
  Pallas kernels  14.9 us (34%)
  waiting for transfers between devices  13.6 us (31%)
  starting transfers between devices  8.21 us (19%)
  local copies, waits for them, and re-layouts  3.74 us (9%)
  other arithmetic  1.8 us (4%)
  between operations  0.81 us (2%)
    pallas_call x8, Pallas kernels, call(): pl.pallas_call(kernel, out_shape=outs, in_specs=specs, out_specs=out_spec...  14.9 us
    ppermute x2, waiting for transfers between devices, from_next_chip(): lax.ppermute(block, ('curve', 'rep'), [(2 * z + 2 + core, 2 * z + core) f...  11.8 us
    ppermute x2, starting transfers between devices, to_next_chip(): lax.ppermute(block, ('curve', 'rep'), [(2 * z + core, 2 * z + 2 + core) f...  4.75 us
    unnamed x6, local copies, waits for them, and re-layouts  3.52 us
    ppermute x2, starting transfers between devices, from_next_chip(): lax.ppermute(block, ('curve', 'rep'), [(2 * z + 2 + core, 2 * z + core) f...  1.99 us
    ppermute x2, waiting for transfers between devices, swap(): return lax.ppermute(block, 'rep', [(0, 1), (1, 0)])  1.78 us
    ppermute x2, starting transfers between devices, swap(): return lax.ppermute(block, 'rep', [(0, 1), (1, 0)])  1.48 us
    add x1, other arithmetic, body(): return mine + jnp.where(core == 0, back, joint).astype(jnp.float32)  1.11 us
  transfers between devices with their start and end apart: 6, of which 3 were waited for; matrix products, arithmetic and copies ran while one was open for 2% of the time, Pallas kernels for 18%

profile of v2, /device:TPU:1, one launch (start us, length us, event | category | flops | bytes accessed | tf_op | source)
XLA Modules:
  0.0 43.0 jit_solution(6012275312778712640)
XLA Ops:
  0.0 4.1 %collective-permute-start = (bf16[32,8192]{1,0:T(8,128)(2,1)}, bf16[32,8192]{1,0:T(8,128)(2,1)S(1)}, u32[]{:S(2)}, u32[]{:S(2)}) collective-permute-start(bf16[32,8192]{1,0:T(8,128)(2,1)} %own.3), channel_id=1, source_target_pairs={{1,5},{5,9},{9,13},{3,7},{7,11},{11,15},{17,21},{21,25},{25,29},{1... | collective-permute-start | bytes 1572872 | tf_op jit(solution)/shard_map/ppermute | solution.py:22
  4.1 0.7 %subtract_select_fusion = s32[128,4]{0,1:T(4,128)S(1)} fusion(s32[128,4]{0,1:T(4,128)} %param.6, s32[]{:T(128)S(6)} %mul.7), kind=kLoop, calls=%fused_computation.1 | loop fusion | flops 1536 | bytes 4100 | tf_op jit(solution)/shard_map/jit(_where)/select_n | solution.py:242
  4.8 0.1 copy.7
  4.9 0.1 reshape.8.index
  5.0 0.0 copy-start.1
  5.0 1.0 %copy-done.1 = bf16[32,8192]{1,0:T(8,128)(2,1)S(1)} copy-done((bf16[32,8192]{1,0:T(8,128)(2,1)S(1)}, bf16[32,8192]{1,0:T(8,128)(2,1)}, u32[]{:S(2)}) %copy-start.1) | copy-done | bytes 524312
  6.0 1.5 %shard_map.48 = (bf16[386,32,128]{2,1,0:T(8,128)(2,1)S(1)}, f32[386,16,128]{2,1,0:T(8,128)S(1)}, bf16[32,8192]{1,0:T(8,128)(2,1)S(1)}) custom-call(bf16[32,8192]{1,0:T(8,128)(2,1)S(1)} %copy-done.1, s32[512]{0:T(512)S(1)} %reshape.8.index), custom_call_target="tpu_custom_call" | custom-call | bytes 1024 | tf_op jit(solution)/shard_map/pallas_call | solution.py:220
  7.5 0.7 %collective-permute-start.2 = (bf16[32,8192]{1,0:T(8,128)(2,1)S(1)}, bf16[32,8192]{1,0:T(8,128)(2,1)S(1)}, u32[]{:S(2)}, u32[]{:S(2)}) collective-permute-start(bf16[32,8192]{1,0:T(8,128)(2,1)S(1)} %get-tuple-element.10), channel_id=1, source_target_pairs={{0,4},{4,8},{8,12},{2,6},{6,10},{10,14},{16,20},{20,24},{24,28},{1... | collective-permute-start | bytes 1572872 | tf_op jit(solution)/shard_map/ppermute | solution.py:22
  8.2 0.0 copy-start
  8.2 2.5 %copy-done = bf16[128,64,320]{0,2,1:T(8,128)(2,1)S(1)} copy-done((bf16[128,64,320]{0,2,1:T(8,128)(2,1)S(1)}, bf16[128,64,320]{0,2,1:T(8,128)(2,1)}, u32[]{:S(2)}) %copy-start) | copy-done | bytes 5242904
  10.7 0.0 copy-start.2
  10.7 3.8 %shard_map.46.factor = bf16[128,64,320]{2,1,0:T(8,128)(2,1)S(1)} custom-call(bf16[64,320,128]{2,1,0:T(8,128)(2,1)S(1)} %bitcast.3), custom_call_target="tpu_custom_call" | custom-call | bytes 14680064 | tf_op jit(solution)/shard_map/pallas_call | solution.py:220
  14.4 0.0 collective-permute-done.arrived.two_odd
  14.5 0.0 copy-done.2
  14.5 0.6 %shard_map.47 = bf16[32,8192]{1,0:T(8,128)(2,1)S(1)} custom-call(s32[1]{0:T(128)} %bitcast.core, bf16[32,8192]{1,0:T(8,128)(2,1)S(1)} %copy-done.2, bf16[32,8192]{1,0:T(8,128)(2,1)S(1)} %collective-permute-done.arrived.two_odd, bf16[128,64,320]{2,1,0:T(8,128)(2,1)S(1)} %shard_map.46.factor, s32[512]{0:T(512)S(1)} %reshape.8.index), custom_call_target="tpu_custom_call" | custom-call | bytes 1024 | tf_op jit(solution)/shard_map/pallas_call | solution.py:220
  15.1 1.0 %collective-permute-start.1 = (bf16[32,8192]{1,0:T(8,128)(2,1)S(1)}, bf16[32,8192]{1,0:T(8,128)(2,1)S(1)}, u32[]{:S(2)}, u32[]{:S(2)}) collective-permute-start(bf16[32,8192]{1,0:T(8,128)(2,1)S(1)} %shard_map.47), channel_id=1, source_target_pairs={{0,1},{1,0},{2,3},{3,2},{4,5},{5,4},{6,7},{7,6},{8,9},{9,8},{10,11... | collective-permute-start | bytes 1572872 | tf_op jit(solution)/shard_map/ppermute | solution.py:35
  16.8 0.0 collective-permute-done.2.two_even
  16.8 0.9 %collective-permute-done.1.one = bf16[32,8192]{1,0:T(8,128)(2,1)S(1)} collective-permute-done((bf16[32,8192]{1,0:T(8,128)(2,1)S(1)}, bf16[32,8192]{1,0:T(8,128)(2,1)S(1)}, u32[]{:S(2)}, u32[]{:S(2)}) %collective-permute-start.1) | collective-permute-done | bytes 524320 | tf_op jit(solution)/shard_map/ppermute | solution.py:35
  17.6 1.4 %shard_map.49.window = bf16[386,32,128]{2,1,0:T(8,128)(2,1)S(1)} custom-call(s32[1]{0:T(128)} %bitcast.core, bf16[32,8192]{1,0:T(8,128)(2,1)S(1)} %collective-permute-done.1.one, bf16[32,8192]{1,0:T(8,128)(2,1)S(1)} %collective-permute-done.2.two_even, bf16[32,8192]{1,0:T(8,128)(2,1)S(1)} %collective-permute-done.arrived.two_odd, ...), custom_call_target="tpu_custom_call", output_to_operand_aliasing={{}: (4, {})} | custom-call | bytes 1024 | tf_op jit(solution)/shard_map/pallas_call | solution.py:220
  19.1 5.6 %shard_map.50 = (f32[32,8192]{1,0:T(8,128)S(1)}, f32[386,16,128]{2,1,0:T(8,128)S(1)}) custom-call(s32[512]{0:T(512)S(1)} %reshape.8.index, s32[1]{0:T(128)S(6)} %copy.10.live, bf16[386,32,128]{2,1,0:T(8,128)(2,1)S(1)} %shard_map.49.window, f32[386,16,128]{2,1,0:T(8,128)S(1)} %get-tuple-element.12.total_in, ...), custom_call_target="tpu_custom_call", output_to_operand_aliasing={{1}: (3, {})} | custom-call | flops 1342177280 | bytes 8388608 | tf_op jit(solution)/shard_map/pallas_call | solution.py:220
  24.7 0.5 %collective-permute-start.3 = (f32[32,8192]{1,0:T(8,128)S(1)}, f32[32,8192]{1,0:T(8,128)S(1)}, u32[]{:S(2)}, u32[]{:S(2)}) collective-permute-start(f32[32,8192]{1,0:T(8,128)S(1)} %get-tuple-element.14), channel_id=1, source_target_pairs={{0,1},{1,0},{2,3},{3,2},{4,5},{5,4},{6,7},{7,6},{8,9},{9,8},{10,11... | collective-permute-start | bytes 3145736 | tf_op jit(solution)/shard_map/ppermute | solution.py:35
  25.1 0.7 %shard_map.52 = bf16[32,8192]{1,0:T(8,128)(2,1)S(1)} custom-call(f32[386,16,128]{2,1,0:T(8,128)S(1)} %get-tuple-element.13.total), custom_call_target="tpu_custom_call" | custom-call | bytes 1024 | tf_op jit(solution)/shard_map/pallas_call | solution.py:220
  25.8 0.7 %collective-permute-start.4 = (bf16[32,8192]{1,0:T(8,128)(2,1)S(1)}, bf16[32,8192]{1,0:T(8,128)(2,1)S(1)}, u32[]{:S(2)}, u32[]{:S(2)}) collective-permute-start(bf16[32,8192]{1,0:T(8,128)(2,1)S(1)} %shard_map.52), channel_id=1, source_target_pairs={{4,0},{8,4},{12,8},{6,2},{10,6},{14,10},{20,16},{24,20},{28,24},{2... | collective-permute-start | bytes 1572872 | tf_op jit(solution)/shard_map/ppermute | solution.py:29
  26.5 0.9 %collective-permute-done.3.across = f32[32,8192]{1,0:T(8,128)S(1)} collective-permute-done((f32[32,8192]{1,0:T(8,128)S(1)}, f32[32,8192]{1,0:T(8,128)S(1)}, u32[]{:S(2)}, u32[]{:S(2)}) %collective-permute-start.3) | collective-permute-done | bytes 1048608 | tf_op jit(solution)/shard_map/ppermute | solution.py:35
  27.4 0.7 %shard_map.53 = bf16[32,8192]{1,0:T(8,128)(2,1)S(1)} custom-call(s32[1]{0:T(128)} %bitcast.core, f32[386,16,128]{2,1,0:T(8,128)S(1)} %get-tuple-element.13.total, f32[32,8192]{1,0:T(8,128)S(1)} %collective-permute-done.3.across), custom_call_target="tpu_custom_call" | custom-call | bytes 1024 | tf_op jit(solution)/shard_map/pallas_call | solution.py:220
  28.1 1.3 %collective-permute-start.5 = (bf16[32,8192]{1,0:T(8,128)(2,1)S(1)}, bf16[32,8192]{1,0:T(8,128)(2,1)S(1)}, u32[]{:S(2)}, u32[]{:S(2)}) collective-permute-start(bf16[32,8192]{1,0:T(8,128)(2,1)S(1)} %shard_map.53), channel_id=1, source_target_pairs={{5,1},{9,5},{13,9},{7,3},{11,7},{15,11},{21,17},{25,21},{29,25},{2... | collective-permute-start | bytes 1572872 | tf_op jit(solution)/shard_map/ppermute | solution.py:29
  29.4 0.7 %shard_map.51 = f32[32,8192]{1,0:T(8,128)S(1)} custom-call(s32[1]{0:T(128)} %bitcast.core, f32[386,16,128]{2,1,0:T(8,128)S(1)} %get-tuple-element.13.total, f32[32,8192]{1,0:T(8,128)S(1)} %collective-permute-done.3.across), custom_call_target="tpu_custom_call" | custom-call | bytes 1024 | tf_op jit(solution)/shard_map/pallas_call | solution.py:220
  30.1 0.0 collective-permute-done.4
  30.2 11.8 %collective-permute-done.5 = bf16[32,8192]{1,0:T(8,128)(2,1)S(1)} collective-permute-done((bf16[32,8192]{1,0:T(8,128)(2,1)S(1)}, bf16[32,8192]{1,0:T(8,128)(2,1)S(1)}, u32[]{:S(2)}, u32[]{:S(2)}) %collective-permute-start.5) | collective-permute-done | bytes 524320 | tf_op jit(solution)/shard_map/ppermute | solution.py:29
  41.9 1.1 %convert_add_fusion = f32[32,8192]{1,0:T(8,128)} fusion(f32[32,8192]{1,0:T(8,128)S(1)} %shard_map.51, bf16[32,8192]{1,0:T(8,128)(2,1)S(1)} %collective-permute-done.4, bf16[32,8192]{1,0:T(8,128)(2,1)S(1)} %collective-permute-done.5, pred[]{:T(512)} %bitcast.2), kind=kLoop, calls=%fused_computation | loop fusion | flops 786432 | bytes 3145729 | tf_op jit(solution)/shard_map/add | solution.py:309
Async XLA Ops:
  0.0 14.4 %collective-permute-start = (bf16[32,8192]{1,0:T(8,128)(2,1)}, bf16[32,8192]{1,0:T(8,128)(2,1)S(1)}, u32[]{:S(2)}, u32[]{:S(2)}) collective-permute-start(bf16[32,8192]{1,0:T(8,128)(2,1)} %own.3), channel_id=1, source_target_pairs={{1,5},{5,9},{9,13},{3,7},{7,11},{11,15},{17,21},{21,25},{25,29},{1... | collective-permute-start | bytes 1572872 | tf_op jit(solution)/shard_map/ppermute | solution.py:22
  5.0 1.0 %copy-start.1 = (bf16[32,8192]{1,0:T(8,128)(2,1)S(1)}, bf16[32,8192]{1,0:T(8,128)(2,1)}, u32[]{:S(2)}) copy-start(bf16[32,8192]{1,0:T(8,128)(2,1)} %own.3) | copy-start | bytes 1572868
  7.5 9.3 %collective-permute-start.2 = (bf16[32,8192]{1,0:T(8,128)(2,1)S(1)}, bf16[32,8192]{1,0:T(8,128)(2,1)S(1)}, u32[]{:S(2)}, u32[]{:S(2)}) collective-permute-start(bf16[32,8192]{1,0:T(8,128)(2,1)S(1)} %get-tuple-element.10), channel_id=1, source_target_pairs={{0,4},{4,8},{8,12},{2,6},{6,10},{10,14},{16,20},{20,24},{24,28},{1... | collective-permute-start | bytes 1572872 | tf_op jit(solution)/shard_map/ppermute | solution.py:22
  8.2 2.5 %copy-start = (bf16[128,64,320]{0,2,1:T(8,128)(2,1)S(1)}, bf16[128,64,320]{0,2,1:T(8,128)(2,1)}, u32[]{:S(2)}) copy-start(bf16[128,64,320]{0,2,1:T(8,128)(2,1)} %param.5) | copy-start | bytes 15728644
  10.7 3.8 %copy-start.2 = (bf16[32,8192]{1,0:T(8,128)(2,1)S(1)}, bf16[32,8192]{1,0:T(8,128)(2,1)}, u32[]{:S(2)}) copy-start(bf16[32,8192]{1,0:T(8,128)(2,1)} %own.3) | copy-start | bytes 1572868
  15.1 2.6 %collective-permute-start.1 = (bf16[32,8192]{1,0:T(8,128)(2,1)S(1)}, bf16[32,8192]{1,0:T(8,128)(2,1)S(1)}, u32[]{:S(2)}, u32[]{:S(2)}) collective-permute-start(bf16[32,8192]{1,0:T(8,128)(2,1)S(1)} %shard_map.47), channel_id=1, source_target_pairs={{0,1},{1,0},{2,3},{3,2},{4,5},{5,4},{6,7},{7,6},{8,9},{9,8},{10,11... | collective-permute-start | bytes 1572872 | tf_op jit(solution)/shard_map/ppermute | solution.py:35
  24.7 2.7 %collective-permute-start.3 = (f32[32,8192]{1,0:T(8,128)S(1)}, f32[32,8192]{1,0:T(8,128)S(1)}, u32[]{:S(2)}, u32[]{:S(2)}) collective-permute-start(f32[32,8192]{1,0:T(8,128)S(1)} %get-tuple-element.14), channel_id=1, source_target_pairs={{0,1},{1,0},{2,3},{3,2},{4,5},{5,4},{6,7},{7,6},{8,9},{9,8},{10,11... | collective-permute-start | bytes 3145736 | tf_op jit(solution)/shard_map/ppermute | solution.py:35
  25.8 4.3 %collective-permute-start.4 = (bf16[32,8192]{1,0:T(8,128)(2,1)S(1)}, bf16[32,8192]{1,0:T(8,128)(2,1)S(1)}, u32[]{:S(2)}, u32[]{:S(2)}) collective-permute-start(bf16[32,8192]{1,0:T(8,128)(2,1)S(1)} %shard_map.52), channel_id=1, source_target_pairs={{4,0},{8,4},{12,8},{6,2},{10,6},{14,10},{20,16},{24,20},{28,24},{2... | collective-permute-start | bytes 1572872 | tf_op jit(solution)/shard_map/ppermute | solution.py:29
  28.1 13.8 %collective-permute-start.5 = (bf16[32,8192]{1,0:T(8,128)(2,1)S(1)}, bf16[32,8192]{1,0:T(8,128)(2,1)S(1)}, u32[]{:S(2)}, u32[]{:S(2)}) collective-permute-start(bf16[32,8192]{1,0:T(8,128)(2,1)S(1)} %shard_map.53), channel_id=1, source_target_pairs={{5,1},{9,5},{13,9},{7,3},{11,7},{15,11},{21,17},{25,21},{29,25},{2... | collective-permute-start | bytes 1572872 | tf_op jit(solution)/shard_map/ppermute | solution.py:29

commit v3 on v2

--- a/solution.py
+++ b/solution.py
@@ -11,6 +11,7 @@
 GROUP = 4
 UNROLL = 16
 PIECES = 4
+SETUP_MIB = 12
 
 VMEM = pl.BlockSpec(memory_space=pltpu.VMEM)
 SMEM = pl.BlockSpec(memory_space=pltpu.SMEM)
@@ -60,7 +61,7 @@
         window[first_block + 2 * t + 1] = half_roll(tile.astype(jnp.float32)).astype(tile.dtype)
         return carry
 
-    lax.fori_loop(0, source.shape[1] // LANES, step, 0, unroll=8)
+    lax.fori_loop(0, source.shape[1] // LANES, step, 0, unroll=32)
 
 
 def collect(total, first_block, target):
@@ -73,18 +74,34 @@
         target[:, lane_tile(t)] = tile
         return carry
 
-    lax.fori_loop(0, target.shape[1] // LANES, step, 0, unroll=8)
-
-
-def turn_kernel(flipped, factor, staged, sems):
-    pieces = staged.shape[0]
-    rows = staged.shape[1]
+    lax.fori_loop(0, target.shape[1] // LANES, step, 0, unroll=32)
+
+
+def again_kernel(own, index, again, sem):
+    copy = pltpu.make_async_copy(own, again, sem)
+    copy.start()
+    copy.wait()
+
+
+def setup_kernel(own, flipped, window, total, factor, staged, sems):
+    pieces, rows = staged.shape[:2]
+    blocks = factor.shape[0]
+    half = total.shape[1]
     copies = [
         pltpu.make_async_copy(flipped.at[pl.ds(i * rows, rows)], staged.at[i], sems.at[i])
         for i in range(pieces)
     ]
     for copy in copies:
         copy.start()
+    spread(own, window, 2 * blocks)
+    window[pl.ds(3 * blocks, 2)] = jnp.zeros((2,) + window.shape[1:], window.dtype)
+
+    def clear(i, carry):
+        total[pl.ds(i * 8, 8)] = jnp.zeros((8, half, LANES), jnp.float32)
+        return carry
+
+    lax.fori_loop(0, 2 * blocks // 8, clear, 0, unroll=4)
+    total[3 * blocks] = jnp.zeros((half, LANES), jnp.float32)
     for i, copy in enumerate(copies):
         copy.wait()
         factor[:, pl.ds(i * rows, rows), :] = jnp.transpose(staged[i], (2, 0, 1))
@@ -98,21 +115,6 @@
     @pl.when(core[0] != 0)
     def _():
         target[...] = arrived[...]
-
-
-def own_kernel(own, index, window, total, again):
-    again[...] = own[...]
-    blocks = own.shape[1] // BS
-    half = total.shape[1]
-    spread(own, window, 2 * blocks)
-    window[pl.ds(3 * blocks, 2)] = jnp.zeros((2,) + window.shape[1:], window.dtype)
-
-    def clear(i, carry):
-        total[pl.ds(i * 8, 8)] = jnp.zeros((8, half, LANES), jnp.float32)
-        return carry
-
-    lax.fori_loop(0, 2 * blocks // 8, clear, 0, unroll=4)
-    total[3 * blocks] = jnp.zeros((half, LANES), jnp.float32)
 
 
 def halo_kernel(core, one, two_even, two_odd, window_in, window):
@@ -201,7 +203,7 @@
         target[:, lane_tile(t)] = tile.astype(target.dtype)
         return carry
 
-    lax.fori_loop(0, target.shape[1] // LANES, step, 0, unroll=8)
+    lax.fori_loop(0, target.shape[1] // LANES, step, 0, unroll=32)
 
 
 def two_kernel(total, target):
@@ -227,6 +229,10 @@
 
 
 LITTLE = pl.CostEstimate(flops=0, bytes_accessed=1024, transcendentals=0)
+
+
+def in_hbm(array):
+    return pltpu.with_memory_space_constraint(array, pltpu.HBM)
 
 
 def params(mib):
@@ -246,33 +252,34 @@
     total_shape = jax.ShapeDtypeStruct((slots, chains // 2, LANES), jnp.float32)
 
     two_odd = to_next_chip(values, 1)
-    window, total, again = call(
-        own_kernel,
-        (window_shape, total_shape, narrow),
-        [VMEM, SMEM],
-        (values, index),
-        out_specs=(VMEM, VMEM, VMEM),
+    again = call(
+        again_kernel,
+        narrow,
+        [HBM, SMEM],
+        (in_hbm(values), index),
+        scratch_shapes=[pltpu.SemaphoreType.DMA],
         compiler_params=params(4),
         cost_estimate=LITTLE,
     )
     two_even = to_next_chip(again, 0)
-    factor = call(
-        turn_kernel,
-        jax.ShapeDtypeStruct(factor.shape, factor.dtype),
-        [HBM],
-        (jnp.transpose(factor, (1, 2, 0)),),
+    window, total, factor = call(
+        setup_kernel,
+        (window_shape, total_shape, jax.ShapeDtypeStruct(factor.shape, factor.dtype)),
+        [VMEM, HBM],
+        (again, in_hbm(jnp.transpose(factor, (1, 2, 0)))),
+        out_specs=(VMEM, VMEM, VMEM),
         scratch_shapes=[
             pltpu.VMEM((PIECES, rows // PIECES, width, blocks), factor.dtype),
             pltpu.SemaphoreType.DMA((PIECES,)),
         ],
-        compiler_params=params(16),
+        compiler_params=params(SETUP_MIB),
         cost_estimate=pl.CostEstimate(flops=0, bytes_accessed=14 * 2**20, transcendentals=0),
     )
     payload = call(
         payload_kernel,
         narrow,
         [SMEM, VMEM, VMEM, VMEM, SMEM],
-        (core, values, two_odd, factor, index),
+        (core, again, two_odd, factor, index),
         compiler_params=params(4), cost_estimate=LITTLE,
     )
     one = swap(payload)

time: 43.3 us -> 40.2 us (0.928)
  local copies, waits for them, and re-layouts: 3.74 us -> 0.22 us
  Pallas kernels: 14.9 us -> 13.5 us
  waiting for transfers between devices: 13.6 us -> 14.7 us
  starting transfers between devices: 8.21 us -> 9.02 us
    unnamed x6 -> x0, local copies, waits for them, and re-layouts: 3.52 us -> none
    pallas_call x8, Pallas kernels: 14.9 us -> 13.5 us  [call(): pl.pallas_call(kernel, out_shape=outs, in_specs=specs, out_specs=out_spec...]
    ppermute x2, starting transfers between devices: 1.48 us -> 2.28 us  [swap(): return lax.ppermute(block, 'rep', [(0, 1), (1, 0)])]
    ppermute x2, waiting for transfers between devices: 11.8 us -> 12.5 us  [from_next_chip(): lax.ppermute(block, ('curve', 'rep'), [(2 * z + 2 + core, 2 * z + core) f...]
    ppermute x2, waiting for transfers between devices: 1.78 us -> 2.22 us  [swap(): return lax.ppermute(block, 'rep', [(0, 1), (1, 0)])]
  transfers between devices with their start and end apart: 6 -> 6, of which waited for: 3 -> 3; matrix products, arithmetic and copies ran while one was open for 2% -> 2% of each run, Pallas kernels for 18% -> 20%
where the time goes in v3:
time: 40.2 us; the launch traced here: 40 us
  waiting for transfers between devices  14.7 us (37%)
  Pallas kernels  13.5 us (34%)
  starting transfers between devices  9.02 us (22%)
  other arithmetic  1.8 us (4%)
  between operations  0.79 us (2%)
    pallas_call x8, Pallas kernels, call(): pl.pallas_call(kernel, out_shape=outs, in_specs=specs, out_specs=out_spec...  13.5 us
    ppermute x2, waiting for transfers between devices, from_next_chip(): lax.ppermute(block, ('curve', 'rep'), [(2 * z + 2 + core, 2 * z + core) f...  12.5 us
    ppermute x2, starting transfers between devices, to_next_chip(): lax.ppermute(block, ('curve', 'rep'), [(2 * z + core, 2 * z + 2 + core) f...  4.75 us
    ppermute x2, starting transfers between devices, swap(): return lax.ppermute(block, 'rep', [(0, 1), (1, 0)])  2.28 us
    ppermute x2, waiting for transfers between devices, swap(): return lax.ppermute(block, 'rep', [(0, 1), (1, 0)])  2.22 us
    ppermute x2, starting transfers between devices, from_next_chip(): lax.ppermute(block, ('curve', 'rep'), [(2 * z + 2 + core, 2 * z + core) f...  1.99 us
    add x1, other arithmetic, body(): return mine + jnp.where(core == 0, back, joint).astype(jnp.float32)  1.11 us
  transfers between devices with their start and end apart: 6, of which 3 were waited for; matrix products, arithmetic and copies ran while one was open for 2% of the time, Pallas kernels for 20%

profile of v3, /device:TPU:1, one launch (start us, length us, event | category | flops | bytes accessed | tf_op | source)
XLA Modules:
  0.0 40.0 jit_solution(4160488029091442899)
XLA Ops:
  0.0 4.1 %collective-permute-start = (bf16[32,8192]{1,0:T(8,128)(2,1)}, bf16[32,8192]{1,0:T(8,128)(2,1)S(1)}, u32[]{:S(2)}, u32[]{:S(2)}) collective-permute-start(bf16[32,8192]{1,0:T(8,128)(2,1)} %own.1), channel_id=1, source_target_pairs={{1,5},{5,9},{9,13},{3,7},{7,11},{11,15},{17,21},{21,25},{25,29},{1... | collective-permute-start | bytes 1572872 | tf_op jit(solution)/shard_map/ppermute | solution.py:23
  4.1 0.7 %subtract_select_fusion = s32[128,4]{0,1:T(4,128)S(1)} fusion(s32[128,4]{0,1:T(4,128)} %param.6, s32[]{:T(128)S(6)} %mul.7), kind=kLoop, calls=%fused_computation.1 | loop fusion | flops 1536 | bytes 4100 | tf_op jit(solution)/shard_map/jit(_where)/select_n | solution.py:248
  4.8 0.1 copy.7
  4.9 0.1 reshape.8.index
  5.0 1.6 %shard_map.46.own = bf16[32,8192]{1,0:T(8,128)(2,1)S(1)} custom-call(bf16[32,8192]{1,0:T(8,128)(2,1)} %own.1, s32[512]{0:T(512)S(1)} %reshape.8.index), custom_call_target="tpu_custom_call" | custom-call | bytes 1024 | tf_op jit(solution)/shard_map/pallas_call | solution.py:222
  6.6 0.7 %collective-permute-start.2 = (bf16[32,8192]{1,0:T(8,128)(2,1)S(1)}, bf16[32,8192]{1,0:T(8,128)(2,1)S(1)}, u32[]{:S(2)}, u32[]{:S(2)}) collective-permute-start(bf16[32,8192]{1,0:T(8,128)(2,1)S(1)} %shard_map.46.own), channel_id=1, source_target_pairs={{0,4},{4,8},{8,12},{2,6},{6,10},{10,14},{16,20},{20,24},{24,28},{1... | collective-permute-start | bytes 1572872 | tf_op jit(solution)/shard_map/ppermute | solution.py:23
  7.3 4.7 %shard_map.47 = (bf16[386,32,128]{2,1,0:T(8,128)(2,1)S(1)}, f32[386,16,128]{2,1,0:T(8,128)S(1)}, bf16[128,64,320]{2,1,0:T(8,128)(2,1)S(1)}) custom-call(bf16[32,8192]{1,0:T(8,128)(2,1)S(1)} %shard_map.46.own, bf16[64,320,128]{2,1,0:T(8,128)(2,1)} %bitcast.3), custom_call_target="tpu_custom_call" | custom-call | bytes 14680064 | tf_op jit(solution)/shard_map/pallas_call | solution.py:222
  12.0 0.0 collective-permute-done.arrived.two_odd
  12.1 0.6 %shard_map.48 = bf16[32,8192]{1,0:T(8,128)(2,1)S(1)} custom-call(s32[1]{0:T(128)} %bitcast.core, bf16[32,8192]{1,0:T(8,128)(2,1)S(1)} %shard_map.46.own, bf16[32,8192]{1,0:T(8,128)(2,1)S(1)} %collective-permute-done.arrived.two_odd, bf16[128,64,320]{2,1,0:T(8,128)(2,1)S(1)} %get-tuple-element.10.factor, s32[512]{0:T(512)S(1)} %reshape.8.index), custom_call_target="tpu_custom_call" | custom-call | bytes 1024 | tf_op jit(solution)/shard_map/pallas_call | solution.py:222
  12.7 1.0 %collective-permute-start.1 = (bf16[32,8192]{1,0:T(8,128)(2,1)S(1)}, bf16[32,8192]{1,0:T(8,128)(2,1)S(1)}, u32[]{:S(2)}, u32[]{:S(2)}) collective-permute-start(bf16[32,8192]{1,0:T(8,128)(2,1)S(1)} %shard_map.48), channel_id=1, source_target_pairs={{0,1},{1,0},{2,3},{3,2},{4,5},{5,4},{6,7},{7,6},{8,9},{9,8},{10,11... | collective-permute-start | bytes 1572872 | tf_op jit(solution)/shard_map/ppermute | solution.py:36
  14.4 0.0 collective-permute-done.2.two_even
  14.4 0.9 %collective-permute-done.1.one = bf16[32,8192]{1,0:T(8,128)(2,1)S(1)} collective-permute-done((bf16[32,8192]{1,0:T(8,128)(2,1)S(1)}, bf16[32,8192]{1,0:T(8,128)(2,1)S(1)}, u32[]{:S(2)}, u32[]{:S(2)}) %collective-permute-start.1) | collective-permute-done | bytes 524320 | tf_op jit(solution)/shard_map/ppermute | solution.py:36
  15.2 0.6 %shard_map.49.window = bf16[386,32,128]{2,1,0:T(8,128)(2,1)S(1)} custom-call(s32[1]{0:T(128)} %bitcast.core, bf16[32,8192]{1,0:T(8,128)(2,1)S(1)} %collective-permute-done.1.one, bf16[32,8192]{1,0:T(8,128)(2,1)S(1)} %collective-permute-done.2.two_even, bf16[32,8192]{1,0:T(8,128)(2,1)S(1)} %collective-permute-done.arrived.two_odd, ...), custom_call_target="tpu_custom_call", output_to_operand_aliasing={{}: (4, {})} | custom-call | bytes 1024 | tf_op jit(solution)/shard_map/pallas_call | solution.py:222
  15.8 5.1 %shard_map.50 = (f32[32,8192]{1,0:T(8,128)S(1)}, f32[386,16,128]{2,1,0:T(8,128)S(1)}) custom-call(s32[512]{0:T(512)S(1)} %reshape.8.index, s32[1]{0:T(128)S(6)} %copy.10.live, bf16[386,32,128]{2,1,0:T(8,128)(2,1)S(1)} %shard_map.49.window, f32[386,16,128]{2,1,0:T(8,128)S(1)} %get-tuple-element.12.total_in, ...), custom_call_target="tpu_custom_call", output_to_operand_aliasing={{1}: (3, {})} | custom-call | flops 1342177280 | bytes 8388608 | tf_op jit(solution)/shard_map/pallas_call | solution.py:222
  20.9 1.3 %collective-permute-start.3 = (f32[32,8192]{1,0:T(8,128)S(1)}, f32[32,8192]{1,0:T(8,128)S(1)}, u32[]{:S(2)}, u32[]{:S(2)}) collective-permute-start(f32[32,8192]{1,0:T(8,128)S(1)} %get-tuple-element.14), channel_id=1, source_target_pairs={{0,1},{1,0},{2,3},{3,2},{4,5},{5,4},{6,7},{7,6},{8,9},{9,8},{10,11... | collective-permute-start | bytes 3145736 | tf_op jit(solution)/shard_map/ppermute | solution.py:36
  22.2 0.2 shard_map.52
  22.4 0.7 %collective-permute-start.4 = (bf16[32,8192]{1,0:T(8,128)(2,1)S(1)}, bf16[32,8192]{1,0:T(8,128)(2,1)S(1)}, u32[]{:S(2)}, u32[]{:S(2)}) collective-permute-start(bf16[32,8192]{1,0:T(8,128)(2,1)S(1)} %shard_map.52), channel_id=1, source_target_pairs={{4,0},{8,4},{12,8},{6,2},{10,6},{14,10},{20,16},{24,20},{28,24},{2... | collective-permute-start | bytes 1572872 | tf_op jit(solution)/shard_map/ppermute | solution.py:30
  23.1 1.3 %collective-permute-done.3.across = f32[32,8192]{1,0:T(8,128)S(1)} collective-permute-done((f32[32,8192]{1,0:T(8,128)S(1)}, f32[32,8192]{1,0:T(8,128)S(1)}, u32[]{:S(2)}, u32[]{:S(2)}) %collective-permute-start.3) | collective-permute-done | bytes 1048608 | tf_op jit(solution)/shard_map/ppermute | solution.py:36
  24.5 0.3 shard_map.53
  24.8 1.3 %collective-permute-start.5 = (bf16[32,8192]{1,0:T(8,128)(2,1)S(1)}, bf16[32,8192]{1,0:T(8,128)(2,1)S(1)}, u32[]{:S(2)}, u32[]{:S(2)}) collective-permute-start(bf16[32,8192]{1,0:T(8,128)(2,1)S(1)} %shard_map.53), channel_id=1, source_target_pairs={{5,1},{9,5},{13,9},{7,3},{11,7},{15,11},{21,17},{25,21},{29,25},{2... | collective-permute-start | bytes 1572872 | tf_op jit(solution)/shard_map/ppermute | solution.py:30
  26.1 0.3 shard_map.51
  26.4 0.0 collective-permute-done.4
  26.4 12.5 %collective-permute-done.5 = bf16[32,8192]{1,0:T(8,128)(2,1)S(1)} collective-permute-done((bf16[32,8192]{1,0:T(8,128)(2,1)S(1)}, bf16[32,8192]{1,0:T(8,128)(2,1)S(1)}, u32[]{:S(2)}, u32[]{:S(2)}) %collective-permute-start.5) | collective-permute-done | bytes 524320 | tf_op jit(solution)/shard_map/ppermute | solution.py:30
  38.9 1.1 %convert_add_fusion = f32[32,8192]{1,0:T(8,128)} fusion(f32[32,8192]{1,0:T(8,128)S(1)} %shard_map.51, bf16[32,8192]{1,0:T(8,128)(2,1)S(1)} %collective-permute-done.4, bf16[32,8192]{1,0:T(8,128)(2,1)S(1)} %collective-permute-done.5, pred[]{:T(512)} %bitcast.2), kind=kLoop, calls=%fused_computation | loop fusion | flops 786432 | bytes 3145729 | tf_op jit(solution)/shard_map/add | solution.py:316
Async XLA Ops:
  0.0 12.0 %collective-permute-start = (bf16[32,8192]{1,0:T(8,128)(2,1)}, bf16[32,8192]{1,0:T(8,128)(2,1)S(1)}, u32[]{:S(2)}, u32[]{:S(2)}) collective-permute-start(bf16[32,8192]{1,0:T(8,128)(2,1)} %own.1), channel_id=1, source_target_pairs={{1,5},{5,9},{9,13},{3,7},{7,11},{11,15},{17,21},{21,25},{25,29},{1... | collective-permute-start | bytes 1572872 | tf_op jit(solution)/shard_map/ppermute | solution.py:23
  6.6 7.7 %collective-permute-start.2 = (bf16[32,8192]{1,0:T(8,128)(2,1)S(1)}, bf16[32,8192]{1,0:T(8,128)(2,1)S(1)}, u32[]{:S(2)}, u32[]{:S(2)}) collective-permute-start(bf16[32,8192]{1,0:T(8,128)(2,1)S(1)} %shard_map.46.own), channel_id=1, source_target_pairs={{0,4},{4,8},{8,12},{2,6},{6,10},{10,14},{16,20},{20,24},{24,28},{1... | collective-permute-start | bytes 1572872 | tf_op jit(solution)/shard_map/ppermute | solution.py:23
  12.7 2.6 %collective-permute-start.1 = (bf16[32,8192]{1,0:T(8,128)(2,1)S(1)}, bf16[32,8192]{1,0:T(8,128)(2,1)S(1)}, u32[]{:S(2)}, u32[]{:S(2)}) collective-permute-start(bf16[32,8192]{1,0:T(8,128)(2,1)S(1)} %shard_map.48), channel_id=1, source_target_pairs={{0,1},{1,0},{2,3},{3,2},{4,5},{5,4},{6,7},{7,6},{8,9},{9,8},{10,11... | collective-permute-start | bytes 1572872 | tf_op jit(solution)/shard_map/ppermute | solution.py:36
  20.9 3.6 %collective-permute-start.3 = (f32[32,8192]{1,0:T(8,128)S(1)}, f32[32,8192]{1,0:T(8,128)S(1)}, u32[]{:S(2)}, u32[]{:S(2)}) collective-permute-start(f32[32,8192]{1,0:T(8,128)S(1)} %get-tuple-element.14), channel_id=1, source_target_pairs={{0,1},{1,0},{2,3},{3,2},{4,5},{5,4},{6,7},{7,6},{8,9},{9,8},{10,11... | collective-permute-start | bytes 3145736 | tf_op jit(solution)/shard_map/ppermute | solution.py:36
  22.4 4.0 %collective-permute-start.4 = (bf16[32,8192]{1,0:T(8,128)(2,1)S(1)}, bf16[32,8192]{1,0:T(8,128)(2,1)S(1)}, u32[]{:S(2)}, u32[]{:S(2)}) collective-permute-start(bf16[32,8192]{1,0:T(8,128)(2,1)S(1)} %shard_map.52), channel_id=1, source_target_pairs={{4,0},{8,4},{12,8},{6,2},{10,6},{14,10},{20,16},{24,20},{28,24},{2... | collective-permute-start | bytes 1572872 | tf_op jit(solution)/shard_map/ppermute | solution.py:30
  24.8 14.1 %collective-permute-start.5 = (bf16[32,8192]{1,0:T(8,128)(2,1)S(1)}, bf16[32,8192]{1,0:T(8,128)(2,1)S(1)}, u32[]{:S(2)}, u32[]{:S(2)}) collective-permute-start(bf16[32,8192]{1,0:T(8,128)(2,1)S(1)} %shard_map.53), channel_id=1, source_target_pairs={{5,1},{9,5},{13,9},{7,3},{11,7},{15,11},{21,17},{25,21},{29,25},{2... | collective-permute-start | bytes 1572872 | tf_op jit(solution)/shard_map/ppermute | solution.py:30

commit v4 on v3

--- a/solution.py
+++ b/solution.py
@@ -77,15 +77,15 @@
     lax.fori_loop(0, target.shape[1] // LANES, step, 0, unroll=32)
 
 
-def again_kernel(own, index, again, sem):
+def again_kernel(own, base, core, again, sem):
     copy = pltpu.make_async_copy(own, again, sem)
     copy.start()
     copy.wait()
 
 
-def setup_kernel(own, flipped, window, total, factor, staged, sems):
+def setup_kernel(own, flipped, window, total, own_map, near_map, own_part, staged, sems):
     pieces, rows = staged.shape[:2]
-    blocks = factor.shape[0]
+    blocks = near_map.shape[0]
     half = total.shape[1]
     copies = [
         pltpu.make_async_copy(flipped.at[pl.ds(i * rows, rows)], staged.at[i], sems.at[i])
@@ -100,14 +100,30 @@
         total[pl.ds(i * 8, 8)] = jnp.zeros((8, half, LANES), jnp.float32)
         return carry
 
-    lax.fori_loop(0, 2 * blocks // 8, clear, 0, unroll=4)
+    lax.fori_loop(0, 3 * blocks // 8, clear, 0, unroll=4)
     total[3 * blocks] = jnp.zeros((half, LANES), jnp.float32)
     for i, copy in enumerate(copies):
         copy.wait()
-        factor[:, pl.ds(i * rows, rows), :] = jnp.transpose(staged[i], (2, 0, 1))
-
-
-def payload_kernel(core, own, arrived, factor, index, target):
+        part = pl.ds(i * rows, rows)
+        own_map[:, part, :] = jnp.transpose(staged[i, :, :BS], (2, 0, 1))
+        near_map[:, part, :] = jnp.transpose(staged[i, :, BS:], (2, 0, 1))
+
+    def start(q, carry):
+        first = q * GROUP
+        mine = [window[2 * blocks + first + b][:, :BS] for b in range(GROUP)]
+        maps = own_map[pl.ds(first, GROUP)].reshape(GROUP * BS, BS)
+        own_part[q] = lax.dot_general(
+            jnp.concatenate(mine, axis=0),
+            maps,
+            (((1,), (1,)), ((), ())),
+            preferred_element_type=jnp.float32,
+        )
+        return carry
+
+    lax.fori_loop(0, blocks // GROUP, start, 0, unroll=8)
+
+
+def payload_kernel(core, own, arrived, factor, target):
     @pl.when(core[0] == 0)
     def _():
         target[...] = own[...]
@@ -117,8 +133,15 @@
         target[...] = arrived[...]
 
 
-def halo_kernel(core, one, two_even, two_odd, window_in, window):
-    spread(one, window, one.shape[1] // BS)
+def main_kernel(
+    core, base, cond, live, one, two_even, two_odd, window_in, total_in, near_map, own_part,
+    out_one, window, total, residuals, index,
+):
+    chains = window.shape[1]
+    half = chains // 2
+    blocks = near_map.shape[0]
+
+    spread(one, window, blocks)
 
     @pl.when(core[0] == 0)
     def _():
@@ -127,14 +150,6 @@
     @pl.when(core[0] != 0)
     def _():
         spread(two_odd, window, 0)
-
-
-def main_kernel(
-    index, live, window, total_in, factor, out_one, total, residuals,
-):
-    chains = window.shape[1]
-    half = chains // 2
-    blocks = factor.shape[0]
 
     low = low_lanes(chains)
     half_low = low_lanes(half)
@@ -149,42 +164,45 @@
         stacked = []
         for b in range(GROUP):
             g = first + b
-            at = [index[g * KN + k] for k in range(KN)]
+            at = []
+            for k in range(KN):
+                place = cond[k, g]
+                place = jnp.where(place >= 0, place - base[0], 3 * blocks)
+                index[g * KN + k] = place
+                at.append(place)
             stacked.append(
                 jnp.concatenate(
                     [
-                        jnp.where(low, window[2 * blocks + g], window[at[0] ^ 1]),
-                        jnp.where(low, window[at[1]], window[at[2] ^ 1]),
-                        window[at[3]][:, :BS],
+                        jnp.where(low, window[at[0]], window[at[1] ^ 1]),
+                        jnp.where(low, window[at[2]], window[at[3] ^ 1]),
                     ],
                     axis=1,
                 )
             )
         stacked = jnp.concatenate(stacked, axis=0)
-        maps = factor[pl.ds(first, GROUP)].reshape(GROUP * BS, BS * (KN + 1))
+        maps = near_map[pl.ds(first, GROUP)].reshape(GROUP * BS, BS * KN)
         residual = lax.dot_general(
             stacked, maps, (((1,), (1,)), ((), ())), preferred_element_type=jnp.float32
         )
+        residual = residual + own_part[q]
         kept = diagonal & (lane_block < live_count - first)
         residuals[q] = jnp.where(kept, -residual, 0.0).astype(jnp.bfloat16)
         return carry
 
     def push(q, carry):
         first = q * GROUP
-        maps = factor[pl.ds(first, GROUP)].reshape(GROUP * BS, BS * (KN + 1))
+        maps = near_map[pl.ds(first, GROUP)].reshape(GROUP * BS, BS * KN)
         terms = jnp.dot(residuals[q], maps, preferred_element_type=jnp.float32)
         for b in range(GROUP):
             g = first + b
             at = [index[g * KN + k] for k in range(KN)]
             a = terms[b * chains : b * chains + half]
             z = terms[b * chains + half : (b + 1) * chains]
-            mine, t0 = cross(half_low, a[:, :LANES], z[:, :LANES])
-            t1, t2 = cross(half_low, a[:, LANES : 2 * LANES], z[:, LANES : 2 * LANES])
-            t3 = jnp.concatenate([a[:, 2 * LANES :], z[:, 2 * LANES :]], axis=1)
+            t0, t1 = cross(half_low, a[:, :LANES], z[:, :LANES])
+            t2, t3 = cross(half_low, a[:, LANES:], z[:, LANES:])
             old = [total[at[k]] for k in range(KN)]
             for k, term in enumerate((t0, t1, t2, t3)):
                 total[at[k]] = old[k] + term
-            total[2 * blocks + g] = mine
         return carry
 
     lax.fori_loop(0, blocks // GROUP, pull, 0, unroll=UNROLL)
@@ -199,7 +217,8 @@
     def step(t, carry):
         even = first_block + 2 * t
         upper, lower = cross(low, total[even], total[even + 1])
-        tile = jnp.concatenate([upper, lower], axis=0) + share * across[:, lane_tile(t)]
+        tile = jnp.concatenate([upper, lower], axis=0)
+        tile = tile + share * across[:, lane_tile(t)].astype(jnp.float32)
         target[:, lane_tile(t)] = tile.astype(target.dtype)
         return carry
 
@@ -214,8 +233,45 @@
     add_across(core, 1, total, across, target, 0)
 
 
-def mine_kernel(core, total, across, target):
-    add_across(core, 0, total, across, target, 2 * (target.shape[1] // BS))
+def mine_kernel(core, total, across, residuals, own_map, target, summed):
+    blocks = own_map.shape[0]
+    chains = target.shape[0]
+    half = chains // 2
+
+    def step(q, carry):
+        first = q * GROUP
+        maps = own_map[pl.ds(first, GROUP)].reshape(GROUP * BS, BS)
+        terms = jnp.dot(residuals[q], maps, preferred_element_type=jnp.float32)
+        for b in range(GROUP):
+            a = terms[b * chains : b * chains + half]
+            z = terms[b * chains + half : (b + 1) * chains]
+            packed = jnp.concatenate([a, z], axis=1)
+            summed[first + b] = total[2 * blocks + first + b] + packed
+        return carry
+
+    lax.fori_loop(0, blocks // GROUP, step, 0, unroll=4)
+    add_across(core, 0, summed, across, target, 0)
+
+
+def final_kernel(core, mine, even, odd, target, ready, sems):
+    parts = sems.shape[0]
+    width = mine.shape[1] // parts
+    copies = []
+    for i in range(parts):
+        lanes = pl.ds(i * width, width)
+
+        @pl.when(core[0] == 0)
+        def _():
+            ready[:, lanes] = mine[:, lanes] + even[:, lanes].astype(jnp.float32)
+
+        @pl.when(core[0] != 0)
+        def _():
+            ready[:, lanes] = mine[:, lanes] + odd[:, lanes].astype(jnp.float32)
+
+        copies.append(pltpu.make_async_copy(ready.at[:, lanes], target.at[:, lanes], sems.at[i]))
+        copies[-1].start()
+    for copy in copies:
+        copy.wait()
 
 
 def call(kernel, outs, specs, args, out_specs=VMEM, **more):
@@ -245,29 +301,37 @@
     slots = 3 * blocks + 2
     position = lax.axis_index(("curve", "rep"))
     core = lax.axis_index("rep").reshape(1)
-    index = jnp.where(cond >= 0, cond - (position - 2) * blocks, 3 * blocks).reshape(-1)
+    base = ((position - 2) * blocks).reshape(1)
     narrow = jax.ShapeDtypeStruct((chains, row_count), jnp.bfloat16)
     wide = jax.ShapeDtypeStruct((chains, row_count), jnp.float32)
     window_shape = jax.ShapeDtypeStruct((slots, chains, LANES), jnp.bfloat16)
     total_shape = jax.ShapeDtypeStruct((slots, chains // 2, LANES), jnp.float32)
 
+    group_shape = (blocks // GROUP, GROUP * chains, GROUP * BS)
+
     two_odd = to_next_chip(values, 1)
     again = call(
         again_kernel,
         narrow,
-        [HBM, SMEM],
-        (in_hbm(values), index),
+        [HBM, SMEM, SMEM],
+        (in_hbm(values), base, core),
         scratch_shapes=[pltpu.SemaphoreType.DMA],
         compiler_params=params(4),
         cost_estimate=LITTLE,
     )
     two_even = to_next_chip(again, 0)
-    window, total, factor = call(
+    window, total, own_map, near_map, own_part = call(
         setup_kernel,
-        (window_shape, total_shape, jax.ShapeDtypeStruct(factor.shape, factor.dtype)),
+        (
+            window_shape,
+            total_shape,
+            jax.ShapeDtypeStruct((blocks, rows, BS), factor.dtype),
+            jax.ShapeDtypeStruct((blocks, rows, width - BS), factor.dtype),
+            jax.ShapeDtypeStruct(group_shape, jnp.float32),
+        ),
         [VMEM, HBM],
         (again, in_hbm(jnp.transpose(factor, (1, 2, 0)))),
-        out_specs=(VMEM, VMEM, VMEM),
+        out_specs=(VMEM,) * 5,
         scratch_shapes=[
             pltpu.VMEM((PIECES, rows // PIECES, width, blocks), factor.dtype),
             pltpu.SemaphoreType.DMA((PIECES,)),
@@ -278,28 +342,21 @@
     payload = call(
         payload_kernel,
         narrow,
-        [SMEM, VMEM, VMEM, VMEM, SMEM],
-        (core, again, two_odd, factor, index),
+        [SMEM, VMEM, VMEM, VMEM],
+        (core, again, two_odd, near_map),
         compiler_params=params(4), cost_estimate=LITTLE,
     )
     one = swap(payload)
-    window = call(
-        halo_kernel,
-        window_shape,
-        [SMEM, VMEM, VMEM, VMEM, VMEM],
-        (core, one, two_even, two_odd, window),
-        input_output_aliases={4: 0}, compiler_params=params(4), cost_estimate=LITTLE
-    )
-    to_one, total = call(
+    to_one, _, total, residuals = call(
         main_kernel,
-        (wide, total_shape),
-        [SMEM, SMEM, VMEM, VMEM, VMEM],
-        (index, live, window, total, factor),
-        out_specs=(VMEM, VMEM),
+        (wide, window_shape, total_shape, jax.ShapeDtypeStruct(group_shape, jnp.bfloat16)),
+        [SMEM] * 4 + [VMEM] * 7,
+        (core, base, jnp.transpose(cond), live, one, two_even, two_odd, window, total, near_map, own_part),
+        out_specs=(VMEM,) * 4,
         scratch_shapes=[
-            pltpu.VMEM((blocks // GROUP, GROUP * chains, GROUP * BS), jnp.bfloat16),
+            pltpu.SMEM((blocks * KN,), jnp.int32),
         ],
-        input_output_aliases={3: 1},
+        input_output_aliases={7: 1, 8: 2},
         compiler_params=params(12),
         cost_estimate=pl.CostEstimate(
             flops=16 * blocks * rows * width * chains,
@@ -310,10 +367,36 @@
     across = swap(to_one)
     to_two = call(two_kernel, narrow, [VMEM], (total,), compiler_params=params(4), cost_estimate=LITTLE)
     back = from_next_chip(to_two, 0)
-    joint = call(joint_kernel, narrow, [SMEM, VMEM, VMEM], (core, total, across), compiler_params=params(4), cost_estimate=LITTLE)
+    joint = call(
+        joint_kernel,
+        narrow,
+        [SMEM, VMEM, VMEM],
+        (core, total, across),
+        compiler_params=params(4),
+        cost_estimate=LITTLE,
+    )
     joint = from_next_chip(joint, 1)
-    mine = call(mine_kernel, wide, [SMEM, VMEM, VMEM], (core, total, across), compiler_params=params(4), cost_estimate=LITTLE)
-    return mine + jnp.where(core == 0, back, joint).astype(jnp.float32)
+    mine = call(
+        mine_kernel,
+        wide,
+        [SMEM, VMEM, VMEM, VMEM, VMEM],
+        (core, total, across, residuals, own_map),
+        scratch_shapes=[pltpu.VMEM((blocks, chains // 2, LANES), jnp.float32)],
+        compiler_params=params(8),
+        cost_estimate=LITTLE,
+    )
+    return call(
+        final_kernel,
+        wide,
+        [SMEM, VMEM, VMEM, VMEM],
+        (core, mine, back, joint),
+        out_specs=HBM,
+        scratch_shapes=[
+            pltpu.VMEM((chains, row_count), jnp.float32),
+            pltpu.SemaphoreType.DMA((PIECES,)),
+        ],
+        compiler_params=params(8),
+    )
 
 
 def solution(mesh):

time: 40.2 us -> 39.7 us (0.988)
  Pallas kernels: 13.5 us -> 16.1 us
  other arithmetic: 1.8 us -> 0 us
  starting transfers between devices: 9.02 us -> 7.89 us
    pallas_call x8, Pallas kernels: 13.5 us -> 16.1 us  [call(): pl.pallas_call(kernel, out_shape=outs, in_specs=specs, out_specs=out_spec...]
    ppermute x2, waiting for transfers between devices: 12.5 us -> 10.2 us  [from_next_chip(): lax.ppermute(block, ('curve', 'rep'), [(2 * z + 2 + core, 2 * z + core) f...]
    ppermute x2, waiting for transfers between devices: 0.01 us -> 1.93 us  [to_next_chip(): lax.ppermute(block, ('curve', 'rep'), [(2 * z + core, 2 * z + 2 + core) f...]
    ppermute x2, starting transfers between devices: 2.28 us -> 1.16 us  [swap(): return lax.ppermute(block, 'rep', [(0, 1), (1, 0)])]
    add x1 -> x0, other arithmetic: 1.11 us -> none  [body(): return mine + jnp.where(core == 0, back, joint).astype(jnp.float32)]
    select_n x1 -> x0, other arithmetic: 0.69 us -> none  [body(): jnp.where(cond >= 0, cond - (position - 2) * blocks, 3 * blocks).reshape(-1)]
  transfers between devices with their start and end apart: 6 -> 6, of which waited for: 3 -> 4; matrix products, arithmetic and copies ran while one was open for 2% -> 0% of each run, Pallas kernels for 20% -> 25%
where the time goes in v4:
time: 39.7 us; the launch traced here: 39.5 us
  Pallas kernels  16.1 us (41%)
  waiting for transfers between devices  14.7 us (37%)
  starting transfers between devices  7.89 us (20%)
  between operations  0.77 us (2%)
    pallas_call x8, Pallas kernels, call(): pl.pallas_call(kernel, out_shape=outs, in_specs=specs, out_specs=out_spec...  16.1 us
    ppermute x2, waiting for transfers between devices, from_next_chip(): lax.ppermute(block, ('curve', 'rep'), [(2 * z + 2 + core, 2 * z + core) f...  10.2 us
    ppermute x2, starting transfers between devices, to_next_chip(): lax.ppermute(block, ('curve', 'rep'), [(2 * z + core, 2 * z + 2 + core) f...  4.74 us
    ppermute x2, waiting for transfers between devices, swap(): return lax.ppermute(block, 'rep', [(0, 1), (1, 0)])  2.59 us
    ppermute x2, starting transfers between devices, from_next_chip(): lax.ppermute(block, ('curve', 'rep'), [(2 * z + 2 + core, 2 * z + core) f...  1.99 us
    ppermute x2, waiting for transfers between devices, to_next_chip(): lax.ppermute(block, ('curve', 'rep'), [(2 * z + core, 2 * z + 2 + core) f...  1.93 us
    ppermute x2, starting transfers between devices, swap(): return lax.ppermute(block, 'rep', [(0, 1), (1, 0)])  1.16 us
  transfers between devices with their start and end apart: 6, of which 4 were waited for; matrix products, arithmetic and copies ran while one was open for 0% of the time, Pallas kernels for 25%

profile of v4, /device:TPU:1, one launch (start us, length us, event | category | flops | bytes accessed | tf_op | source)
XLA Modules:
  0.0 39.5 jit_solution(8906671783601640849)
XLA Ops:
  0.0 4.0 %collective-permute-start = (bf16[32,8192]{1,0:T(8,128)(2,1)}, bf16[32,8192]{1,0:T(8,128)(2,1)S(1)}, u32[]{:S(2)}, u32[]{:S(2)}) collective-permute-start(bf16[32,8192]{1,0:T(8,128)(2,1)} %own.1), channel_id=1, source_target_pairs={{1,5},{5,9},{9,13},{3,7},{7,11},{11,15},{17,21},{21,25},{25,29},{1... | collective-permute-start | bytes 1572872 | tf_op jit(solution)/shard_map/ppermute | solution.py:23
  4.1 1.1 %shard_map.46.own = bf16[32,8192]{1,0:T(8,128)(2,1)S(1)} custom-call(bf16[32,8192]{1,0:T(8,128)(2,1)} %own.1, s32[1]{0:T(128)} %bitcast.1.base, s32[1]{0:T(128)} %bitcast.core), custom_call_target="tpu_custom_call" | custom-call | bytes 1024 | tf_op jit(solution)/shard_map/pallas_call | solution.py:278
  5.1 0.7 %collective-permute-start.2 = (bf16[32,8192]{1,0:T(8,128)(2,1)S(1)}, bf16[32,8192]{1,0:T(8,128)(2,1)S(1)}, u32[]{:S(2)}, u32[]{:S(2)}) collective-permute-start(bf16[32,8192]{1,0:T(8,128)(2,1)S(1)} %shard_map.46.own), channel_id=1, source_target_pairs={{0,4},{4,8},{8,12},{2,6},{6,10},{10,14},{16,20},{20,24},{24,28},{1... | collective-permute-start | bytes 1572872 | tf_op jit(solution)/shard_map/ppermute | solution.py:23
  5.8 5.5 %shard_map.47 = (bf16[386,32,128]{2,1,0:T(8,128)(2,1)S(1)}, f32[386,16,128]{2,1,0:T(8,128)S(1)}, bf16[128,64,64]{2,1,0:T(8,128)(2,1)S(1)}, bf16[128,64,256]{2,1,0:T(8,128)(2,1)S(1)}, f32[32,128,256]{2,1,0:T(8,128)S(1)}) custom-call(bf16[32,8192]{1,0:T(8,128)(2,1)S(1)} %shard_map.46.own, bf16[64,320,128]{2,1,0:T(8,128)(2,1)} %bitcast.5), custom_call_target="tpu_custom_call" | custom-call | bytes 14680064 | tf_op jit(solution)/shard_map/pallas_call | solution.py:278
  11.4 0.0 copy-start
  11.4 1.9 %collective-permute-done.arrived.two_odd = bf16[32,8192]{1,0:T(8,128)(2,1)S(1)} collective-permute-done((bf16[32,8192]{1,0:T(8,128)(2,1)}, bf16[32,8192]{1,0:T(8,128)(2,1)S(1)}, u32[]{:S(2)}, u32[]{:S(2)}) %collective-permute-start) | collective-permute-done | bytes 524320 | tf_op jit(solution)/shard_map/ppermute | solution.py:23
  13.3 0.1 collective-permute-start.1
  14.1 0.0 collective-permute-done.2.two_even
  14.1 1.2 %collective-permute-done.1.one = bf16[32,8192]{1,0:T(8,128)(2,1)S(1)} collective-permute-done((bf16[32,8192]{1,0:T(8,128)(2,1)S(1)}, bf16[32,8192]{1,0:T(8,128)(2,1)S(1)}, u32[]{:S(2)}, u32[]{:S(2)}) %collective-permute-start.1) | collective-permute-done | bytes 524320 | tf_op jit(solution)/shard_map/ppermute | solution.py:36
  15.3 0.0 copy-done
  15.3 5.2 %shard_map.49 = (f32[32,8192]{1,0:T(8,128)S(1)}, bf16[386,32,128]{2,1,0:T(8,128)(2,1)S(1)}, f32[386,16,128]{2,1,0:T(8,128)S(1)}, bf16[32,128,256]{2,1,0:T(8,128)(2,1)S(1)}) custom-call(s32[1]{0:T(128)} %bitcast.core, s32[1]{0:T(128)} %bitcast.1.base, s32[4,128]{1,0:T(4,128)S(1)} %bitcast.4, ...), custom_call_target="tpu_custom_call", output_to_operand_aliasing={{1}: (7, {}), {2}: (8, {})} | custom-call | flops 1342177280 | bytes 8388608 | tf_op jit(solution)/shard_map/pallas_call | solution.py:278
  20.6 1.1 %collective-permute-start.3 = (f32[32,8192]{1,0:T(8,128)S(1)}, f32[32,8192]{1,0:T(8,128)S(1)}, u32[]{:S(2)}, u32[]{:S(2)}) collective-permute-start(f32[32,8192]{1,0:T(8,128)S(1)} %get-tuple-element.18), channel_id=1, source_target_pairs={{0,1},{1,0},{2,3},{3,2},{4,5},{5,4},{6,7},{7,6},{8,9},{9,8},{10,11... | collective-permute-start | bytes 3145736 | tf_op jit(solution)/shard_map/ppermute | solution.py:36
  21.6 0.2 shard_map.51
  21.9 0.7 %collective-permute-start.4 = (bf16[32,8192]{1,0:T(8,128)(2,1)S(1)}, bf16[32,8192]{1,0:T(8,128)(2,1)S(1)}, u32[]{:S(2)}, u32[]{:S(2)}) collective-permute-start(bf16[32,8192]{1,0:T(8,128)(2,1)S(1)} %shard_map.51), channel_id=1, source_target_pairs={{4,0},{8,4},{12,8},{6,2},{10,6},{14,10},{20,16},{24,20},{28,24},{2... | collective-permute-start | bytes 1572872 | tf_op jit(solution)/shard_map/ppermute | solution.py:30
  22.6 1.3 %collective-permute-done.3.across = f32[32,8192]{1,0:T(8,128)S(1)} collective-permute-done((f32[32,8192]{1,0:T(8,128)S(1)}, f32[32,8192]{1,0:T(8,128)S(1)}, u32[]{:S(2)}, u32[]{:S(2)}) %collective-permute-start.3) | collective-permute-done | bytes 1048608 | tf_op jit(solution)/shard_map/ppermute | solution.py:36
  23.9 0.3 shard_map.52
  24.2 1.3 %collective-permute-start.5 = (bf16[32,8192]{1,0:T(8,128)(2,1)S(1)}, bf16[32,8192]{1,0:T(8,128)(2,1)S(1)}, u32[]{:S(2)}, u32[]{:S(2)}) collective-permute-start(bf16[32,8192]{1,0:T(8,128)(2,1)S(1)} %shard_map.52), channel_id=1, source_target_pairs={{5,1},{9,5},{13,9},{7,3},{11,7},{15,11},{21,17},{25,21},{29,25},{2... | collective-permute-start | bytes 1572872 | tf_op jit(solution)/shard_map/ppermute | solution.py:30
  25.6 2.7 %shard_map.50.mine = f32[32,8192]{1,0:T(8,128)S(1)} custom-call(s32[1]{0:T(128)} %bitcast.core, f32[386,16,128]{2,1,0:T(8,128)S(1)} %get-tuple-element.17.total, f32[32,8192]{1,0:T(8,128)S(1)} %collective-permute-done.3.across, bf16[32,128,256]{2,1,0:T(8,128)(2,1)S(1)} %get-tuple-element.19.residuals, bf16[128,64,64]{2,1,0:T(8,128)(2,1)S(1)} %get-tuple-element.20.own_map), custom_call_target="tpu_custom_call" | custom-call | bytes 1024 | tf_op jit(solution)/shard_map/pallas_call | solution.py:278
  28.2 0.0 collective-permute-done.4.even
  28.2 10.2 %collective-permute-done.5.odd = bf16[32,8192]{1,0:T(8,128)(2,1)S(1)} collective-permute-done((bf16[32,8192]{1,0:T(8,128)(2,1)S(1)}, bf16[32,8192]{1,0:T(8,128)(2,1)S(1)}, u32[]{:S(2)}, u32[]{:S(2)}) %collective-permute-start.5) | collective-permute-done | bytes 524320 | tf_op jit(solution)/shard_map/ppermute | solution.py:30
  38.4 1.0 %shard_map.53 = f32[32,8192]{1,0:T(8,128)} custom-call(s32[1]{0:T(128)} %bitcast.core, f32[32,8192]{1,0:T(8,128)S(1)} %shard_map.50.mine, bf16[32,8192]{1,0:T(8,128)(2,1)S(1)} %collective-permute-done.4.even, bf16[32,8192]{1,0:T(8,128)(2,1)S(1)} %collective-permute-done.5.odd), custom_call_target="tpu_custom_call" | custom-call | tf_op jit(solution)/shard_map/pallas_call | solution.py:278
  (1 shorter events, 0.0 us)
Async XLA Ops:
  0.0 13.3 %collective-permute-start = (bf16[32,8192]{1,0:T(8,128)(2,1)}, bf16[32,8192]{1,0:T(8,128)(2,1)S(1)}, u32[]{:S(2)}, u32[]{:S(2)}) collective-permute-start(bf16[32,8192]{1,0:T(8,128)(2,1)} %own.1), channel_id=1, source_target_pairs={{1,5},{5,9},{9,13},{3,7},{7,11},{11,15},{17,21},{21,25},{25,29},{1... | collective-permute-start | bytes 1572872 | tf_op jit(solution)/shard_map/ppermute | solution.py:23
  5.1 8.9 %collective-permute-start.2 = (bf16[32,8192]{1,0:T(8,128)(2,1)S(1)}, bf16[32,8192]{1,0:T(8,128)(2,1)S(1)}, u32[]{:S(2)}, u32[]{:S(2)}) collective-permute-start(bf16[32,8192]{1,0:T(8,128)(2,1)S(1)} %shard_map.46.own), channel_id=1, source_target_pairs={{0,4},{4,8},{8,12},{2,6},{6,10},{10,14},{16,20},{20,24},{24,28},{1... | collective-permute-start | bytes 1572872 | tf_op jit(solution)/shard_map/ppermute | solution.py:23
  11.4 4.0 %copy-start = (s32[128,4]{0,1:T(4,128)S(1)}, s32[128,4]{0,1:T(4,128)}, u32[]{:S(2)}) copy-start(s32[128,4]{0,1:T(4,128)} %param.6) | copy-start | bytes 6148
  13.3 2.0 %collective-permute-start.1 = (bf16[32,8192]{1,0:T(8,128)(2,1)S(1)}, bf16[32,8192]{1,0:T(8,128)(2,1)S(1)}, u32[]{:S(2)}, u32[]{:S(2)}) collective-permute-start(bf16[32,8192]{1,0:T(8,128)(2,1)S(1)} %shard_map.48), channel_id=1, source_target_pairs={{0,1},{1,0},{2,3},{3,2},{4,5},{5,4},{6,7},{7,6},{8,9},{9,8},{10,11... | collective-permute-start | bytes 1572872 | tf_op jit(solution)/shard_map/ppermute | solution.py:36
  20.6 3.4 %collective-permute-start.3 = (f32[32,8192]{1,0:T(8,128)S(1)}, f32[32,8192]{1,0:T(8,128)S(1)}, u32[]{:S(2)}, u32[]{:S(2)}) collective-permute-start(f32[32,8192]{1,0:T(8,128)S(1)} %get-tuple-element.18), channel_id=1, source_target_pairs={{0,1},{1,0},{2,3},{3,2},{4,5},{5,4},{6,7},{7,6},{8,9},{9,8},{10,11... | collective-permute-start | bytes 3145736 | tf_op jit(solution)/shard_map/ppermute | solution.py:36
  21.9 6.3 %collective-permute-start.4 = (bf16[32,8192]{1,0:T(8,128)(2,1)S(1)}, bf16[32,8192]{1,0:T(8,128)(2,1)S(1)}, u32[]{:S(2)}, u32[]{:S(2)}) collective-permute-start(bf16[32,8192]{1,0:T(8,128)(2,1)S(1)} %shard_map.51), channel_id=1, source_target_pairs={{4,0},{8,4},{12,8},{6,2},{10,6},{14,10},{20,16},{24,20},{28,24},{2... | collective-permute-start | bytes 1572872 | tf_op jit(solution)/shard_map/ppermute | solution.py:30
  24.2 14.2 %collective-permute-start.5 = (bf16[32,8192]{1,0:T(8,128)(2,1)S(1)}, bf16[32,8192]{1,0:T(8,128)(2,1)S(1)}, u32[]{:S(2)}, u32[]{:S(2)}) collective-permute-start(bf16[32,8192]{1,0:T(8,128)(2,1)S(1)} %shard_map.52), channel_id=1, source_target_pairs={{5,1},{9,5},{13,9},{7,3},{11,7},{15,11},{21,17},{25,21},{29,25},{2... | collective-permute-start | bytes 1572872 | tf_op jit(solution)/shard_map/ppermute | solution.py:30

commit v5 on v4

--- a/solution.py
+++ b/solution.py
@@ -9,7 +9,7 @@
 KN = 4
 LANES = 128
 GROUP = 4
-UNROLL = 16
+LAG = 4
 PIECES = 4
 SETUP_MIB = 12
 
@@ -61,7 +61,7 @@
         window[first_block + 2 * t + 1] = half_roll(tile.astype(jnp.float32)).astype(tile.dtype)
         return carry
 
-    lax.fori_loop(0, source.shape[1] // LANES, step, 0, unroll=32)
+    lax.fori_loop(0, source.shape[1] // LANES, step, 0, unroll=64)
 
 
 def collect(total, first_block, target):
@@ -74,10 +74,10 @@
         target[:, lane_tile(t)] = tile
         return carry
 
-    lax.fori_loop(0, target.shape[1] // LANES, step, 0, unroll=32)
-
-
-def again_kernel(own, base, core, again, sem):
+    lax.fori_loop(0, target.shape[1] // LANES, step, 0, unroll=64)
+
+
+def again_kernel(own, again, sem):
     copy = pltpu.make_async_copy(own, again, sem)
     copy.start()
     copy.wait()
@@ -123,31 +123,35 @@
     lax.fori_loop(0, blocks // GROUP, start, 0, unroll=8)
 
 
-def payload_kernel(core, own, arrived, factor, target):
-    @pl.when(core[0] == 0)
+def payload_kernel(own, arrived, factor, target):
+    core = lax.axis_index("rep")
+
+    @pl.when(core == 0)
     def _():
         target[...] = own[...]
 
-    @pl.when(core[0] != 0)
+    @pl.when(core != 0)
     def _():
         target[...] = arrived[...]
 
 
 def main_kernel(
-    core, base, cond, live, one, two_even, two_odd, window_in, total_in, near_map, own_part,
+    cond, live, one, two_even, two_odd, window_in, total_in, near_map, own_part,
     out_one, window, total, residuals, index,
 ):
     chains = window.shape[1]
     half = chains // 2
     blocks = near_map.shape[0]
 
+    core = lax.axis_index("rep")
+    base = (lax.axis_index("curve") * 2 + core - 2) * blocks
     spread(one, window, blocks)
 
-    @pl.when(core[0] == 0)
+    @pl.when(core == 0)
     def _():
         spread(two_even, window, 0)
 
-    @pl.when(core[0] != 0)
+    @pl.when(core != 0)
     def _():
         spread(two_odd, window, 0)
 
@@ -159,7 +163,7 @@
     diagonal = row_block == lane_block
     live_count = live[0]
 
-    def pull(q, carry):
+    def pull(q):
         first = q * GROUP
         stacked = []
         for b in range(GROUP):
@@ -167,7 +171,7 @@
             at = []
             for k in range(KN):
                 place = cond[k, g]
-                place = jnp.where(place >= 0, place - base[0], 3 * blocks)
+                place = jnp.where(place >= 0, place - base, 3 * blocks)
                 index[g * KN + k] = place
                 at.append(place)
             stacked.append(
@@ -187,9 +191,8 @@
         residual = residual + own_part[q]
         kept = diagonal & (lane_block < live_count - first)
         residuals[q] = jnp.where(kept, -residual, 0.0).astype(jnp.bfloat16)
-        return carry
-
-    def push(q, carry):
+
+    def push(q):
         first = q * GROUP
         maps = near_map[pl.ds(first, GROUP)].reshape(GROUP * BS, BS * KN)
         terms = jnp.dot(residuals[q], maps, preferred_element_type=jnp.float32)
@@ -203,16 +206,19 @@
             old = [total[at[k]] for k in range(KN)]
             for k, term in enumerate((t0, t1, t2, t3)):
                 total[at[k]] = old[k] + term
-        return carry
-
-    lax.fori_loop(0, blocks // GROUP, pull, 0, unroll=UNROLL)
-    lax.fori_loop(0, blocks // GROUP, push, 0, unroll=UNROLL)
+
+    groups = blocks // GROUP
+    for q in range(groups + LAG):
+        if q < groups:
+            pull(q)
+        if q >= LAG:
+            push(q - LAG)
     collect(total, blocks, out_one)
 
 
-def add_across(core, keeper, total, across, target, first_block):
+def add_across(keeper, total, across, target, first_block):
     low = low_lanes(total.shape[1])
-    share = jnp.where(core[0] == keeper, 1.0, 0.0)
+    share = jnp.where(lax.axis_index("rep") == keeper, 1.0, 0.0)
 
     def step(t, carry):
         even = first_block + 2 * t
@@ -222,18 +228,18 @@
         target[:, lane_tile(t)] = tile.astype(target.dtype)
         return carry
 
-    lax.fori_loop(0, target.shape[1] // LANES, step, 0, unroll=32)
+    lax.fori_loop(0, target.shape[1] // LANES, step, 0, unroll=64)
 
 
 def two_kernel(total, target):
     collect(total, 0, target)
 
 
-def joint_kernel(core, total, across, target):
-    add_across(core, 1, total, across, target, 0)
-
-
-def mine_kernel(core, total, across, residuals, own_map, target, summed):
+def joint_kernel(total, across, target):
+    add_across(1, total, across, target, 0)
+
+
+def mine_kernel(total, across, residuals, own_map, target, summed):
     blocks = own_map.shape[0]
     chains = target.shape[0]
     half = chains // 2
@@ -250,21 +256,22 @@
         return carry
 
     lax.fori_loop(0, blocks // GROUP, step, 0, unroll=4)
-    add_across(core, 0, summed, across, target, 0)
-
-
-def final_kernel(core, mine, even, odd, target, ready, sems):
+    add_across(0, summed, across, target, 0)
+
+
+def final_kernel(mine, even, odd, target, ready, sems):
+    core = lax.axis_index("rep")
     parts = sems.shape[0]
     width = mine.shape[1] // parts
     copies = []
     for i in range(parts):
         lanes = pl.ds(i * width, width)
 
-        @pl.when(core[0] == 0)
+        @pl.when(core == 0)
         def _():
             ready[:, lanes] = mine[:, lanes] + even[:, lanes].astype(jnp.float32)
 
-        @pl.when(core[0] != 0)
+        @pl.when(core != 0)
         def _():
             ready[:, lanes] = mine[:, lanes] + odd[:, lanes].astype(jnp.float32)
 
@@ -299,9 +306,6 @@
     chains, row_count = values.shape
     blocks, rows, width = factor.shape
     slots = 3 * blocks + 2
-    position = lax.axis_index(("curve", "rep"))
-    core = lax.axis_index("rep").reshape(1)
-    base = ((position - 2) * blocks).reshape(1)
     narrow = jax.ShapeDtypeStruct((chains, row_count), jnp.bfloat16)
     wide = jax.ShapeDtypeStruct((chains, row_count), jnp.float32)
     window_shape = jax.ShapeDtypeStruct((slots, chains, LANES), jnp.bfloat16)
@@ -313,8 +317,8 @@
     again = call(
         again_kernel,
         narrow,
-        [HBM, SMEM, SMEM],
-        (in_hbm(values), base, core),
+        [HBM],
+        (in_hbm(values),),
         scratch_shapes=[pltpu.SemaphoreType.DMA],
         compiler_params=params(4),
         cost_estimate=LITTLE,
@@ -342,21 +346,21 @@
     payload = call(
         payload_kernel,
         narrow,
-        [SMEM, VMEM, VMEM, VMEM],
-        (core, again, two_odd, near_map),
+        [VMEM, VMEM, VMEM],
+        (again, two_odd, near_map),
         compiler_params=params(4), cost_estimate=LITTLE,
     )
     one = swap(payload)
     to_one, _, total, residuals = call(
         main_kernel,
         (wide, window_shape, total_shape, jax.ShapeDtypeStruct(group_shape, jnp.bfloat16)),
-        [SMEM] * 4 + [VMEM] * 7,
-        (core, base, jnp.transpose(cond), live, one, two_even, two_odd, window, total, near_map, own_part),
+        [SMEM] * 2 + [VMEM] * 7,
+        (jnp.transpose(cond), live, one, two_even, two_odd, window, total, near_map, own_part),
         out_specs=(VMEM,) * 4,
         scratch_shapes=[
             pltpu.SMEM((blocks * KN,), jnp.int32),
         ],
-        input_output_aliases={7: 1, 8: 2},
+        input_output_aliases={5: 1, 6: 2},
         compiler_params=params(12),
         cost_estimate=pl.CostEstimate(
             flops=16 * blocks * rows * width * chains,
@@ -370,8 +374,8 @@
     joint = call(
         joint_kernel,
         narrow,
-        [SMEM, VMEM, VMEM],
-        (core, total, across),
+        [VMEM, VMEM],
+        (total, across),
         compiler_params=params(4),
         cost_estimate=LITTLE,
     )
@@ -379,8 +383,8 @@
     mine = call(
         mine_kernel,
         wide,
-        [SMEM, VMEM, VMEM, VMEM, VMEM],
-        (core, total, across, residuals, own_map),
+        [VMEM, VMEM, VMEM, VMEM],
+        (total, across, residuals, own_map),
         scratch_shapes=[pltpu.VMEM((blocks, chains // 2, LANES), jnp.float32)],
         compiler_params=params(8),
         cost_estimate=LITTLE,
@@ -388,8 +392,8 @@
     return call(
         final_kernel,
         wide,
-        [SMEM, VMEM, VMEM, VMEM],
-        (core, mine, back, joint),
+        [VMEM, VMEM, VMEM],
+        (mine, back, joint),
         out_specs=HBM,
         scratch_shapes=[
             pltpu.VMEM((chains, row_count), jnp.float32),

time: 39.7 us -> 38.3 us (0.965)
  Pallas kernels: 16.1 us -> 14.7 us
    pallas_call x8, Pallas kernels: 16.1 us -> 14.7 us  [call(): pl.pallas_call(kernel, out_shape=outs, in_specs=specs, out_specs=out_spec...]
where the time goes in v5:
time: 38.3 us; the launch traced here: 38.1 us
  Pallas kernels  14.7 us (38%)
  waiting for transfers between devices  14.7 us (38%)
  starting transfers between devices  7.91 us (21%)
  between operations  0.77 us (2%)
    pallas_call x8, Pallas kernels, call(): pl.pallas_call(kernel, out_shape=outs, in_specs=specs, out_specs=out_spec...  14.7 us
    ppermute x2, waiting for transfers between devices, from_next_chip(): lax.ppermute(block, ('curve', 'rep'), [(2 * z + 2 + core, 2 * z + core) f...  10.2 us
    ppermute x2, starting transfers between devices, to_next_chip(): lax.ppermute(block, ('curve', 'rep'), [(2 * z + core, 2 * z + 2 + core) f...  4.74 us
    ppermute x2, waiting for transfers between devices, swap(): return lax.ppermute(block, 'rep', [(0, 1), (1, 0)])  2.66 us
    ppermute x2, starting transfers between devices, from_next_chip(): lax.ppermute(block, ('curve', 'rep'), [(2 * z + 2 + core, 2 * z + core) f...  1.99 us
    ppermute x2, waiting for transfers between devices, to_next_chip(): lax.ppermute(block, ('curve', 'rep'), [(2 * z + core, 2 * z + 2 + core) f...  1.85 us
    ppermute x2, starting transfers between devices, swap(): return lax.ppermute(block, 'rep', [(0, 1), (1, 0)])  1.18 us
  transfers between devices with their start and end apart: 6, of which 4 were waited for; matrix products, arithmetic and copies ran while one was open for 0% of the time, Pallas kernels for 25%

profile of v5, /device:TPU:1, one launch (start us, length us, event | category | flops | bytes accessed | tf_op | source)
XLA Modules:
  0.0 38.1 jit_solution(4498125499576473721)
XLA Ops:
  0.0 4.0 %collective-permute-start = (bf16[32,8192]{1,0:T(8,128)(2,1)}, bf16[32,8192]{1,0:T(8,128)(2,1)S(1)}, u32[]{:S(2)}, u32[]{:S(2)}) collective-permute-start(bf16[32,8192]{1,0:T(8,128)(2,1)} %own.1), channel_id=1, source_target_pairs={{1,5},{5,9},{9,13},{3,7},{7,11},{11,15},{17,21},{21,25},{25,29},{1... | collective-permute-start | bytes 1572872 | tf_op jit(solution)/shard_map/ppermute | solution.py:23
  4.1 1.1 %shard_map.46.own = bf16[32,8192]{1,0:T(8,128)(2,1)S(1)} custom-call(bf16[32,8192]{1,0:T(8,128)(2,1)} %own.1), custom_call_target="tpu_custom_call" | custom-call | bytes 1024 | tf_op jit(solution)/shard_map/pallas_call | solution.py:285
  5.1 0.7 %collective-permute-start.2 = (bf16[32,8192]{1,0:T(8,128)(2,1)S(1)}, bf16[32,8192]{1,0:T(8,128)(2,1)S(1)}, u32[]{:S(2)}, u32[]{:S(2)}) collective-permute-start(bf16[32,8192]{1,0:T(8,128)(2,1)S(1)} %shard_map.46.own), channel_id=1, source_target_pairs={{0,4},{4,8},{8,12},{2,6},{6,10},{10,14},{16,20},{20,24},{24,28},{1... | collective-permute-start | bytes 1572872 | tf_op jit(solution)/shard_map/ppermute | solution.py:23
  5.8 5.6 %shard_map.47 = (bf16[386,32,128]{2,1,0:T(8,128)(2,1)S(1)}, f32[386,16,128]{2,1,0:T(8,128)S(1)}, bf16[128,64,64]{2,1,0:T(8,128)(2,1)S(1)}, bf16[128,64,256]{2,1,0:T(8,128)(2,1)S(1)}, f32[32,128,256]{2,1,0:T(8,128)S(1)}) custom-call(bf16[32,8192]{1,0:T(8,128)(2,1)S(1)} %shard_map.46.own, bf16[64,320,128]{2,1,0:T(8,128)(2,1)} %bitcast.3), custom_call_target="tpu_custom_call" | custom-call | bytes 14680064 | tf_op jit(solution)/shard_map/pallas_call | solution.py:285
  11.4 0.0 copy-start
  11.5 1.9 %collective-permute-done.arrived.two_odd = bf16[32,8192]{1,0:T(8,128)(2,1)S(1)} collective-permute-done((bf16[32,8192]{1,0:T(8,128)(2,1)}, bf16[32,8192]{1,0:T(8,128)(2,1)S(1)}, u32[]{:S(2)}, u32[]{:S(2)}) %collective-permute-start) | collective-permute-done | bytes 524320 | tf_op jit(solution)/shard_map/ppermute | solution.py:23
  13.4 0.1 collective-permute-start.1
  14.1 0.0 collective-permute-done.2.two_even
  14.1 1.2 %collective-permute-done.1.one = bf16[32,8192]{1,0:T(8,128)(2,1)S(1)} collective-permute-done((bf16[32,8192]{1,0:T(8,128)(2,1)S(1)}, bf16[32,8192]{1,0:T(8,128)(2,1)S(1)}, u32[]{:S(2)}, u32[]{:S(2)}) %collective-permute-start.1) | collective-permute-done | bytes 524320 | tf_op jit(solution)/shard_map/ppermute | solution.py:36
  15.3 0.0 copy-done
  15.3 4.0 %shard_map.49 = (f32[32,8192]{1,0:T(8,128)S(1)}, bf16[386,32,128]{2,1,0:T(8,128)(2,1)S(1)}, f32[386,16,128]{2,1,0:T(8,128)S(1)}, bf16[32,128,256]{2,1,0:T(8,128)(2,1)S(1)}) custom-call(s32[4,128]{1,0:T(4,128)S(1)} %bitcast.2, s32[1]{0:T(128)S(6)} %copy.9.live, ...), custom_call_target="tpu_custom_call", output_to_operand_aliasing={{1}: (5, {}), {2}: (6, {})} | custom-call | flops 1342177280 | bytes 8388608 | tf_op jit(solution)/shard_map/pallas_call | solution.py:285
  19.3 1.1 %collective-permute-start.3 = (f32[32,8192]{1,0:T(8,128)S(1)}, f32[32,8192]{1,0:T(8,128)S(1)}, u32[]{:S(2)}, u32[]{:S(2)}) collective-permute-start(f32[32,8192]{1,0:T(8,128)S(1)} %get-tuple-element.18), channel_id=1, source_target_pairs={{0,1},{1,0},{2,3},{3,2},{4,5},{5,4},{6,7},{7,6},{8,9},{9,8},{10,11... | collective-permute-start | bytes 3145736 | tf_op jit(solution)/shard_map/ppermute | solution.py:36
  20.4 0.2 shard_map.51
  20.6 0.7 %collective-permute-start.4 = (bf16[32,8192]{1,0:T(8,128)(2,1)S(1)}, bf16[32,8192]{1,0:T(8,128)(2,1)S(1)}, u32[]{:S(2)}, u32[]{:S(2)}) collective-permute-start(bf16[32,8192]{1,0:T(8,128)(2,1)S(1)} %shard_map.51), channel_id=1, source_target_pairs={{4,0},{8,4},{12,8},{6,2},{10,6},{14,10},{20,16},{24,20},{28,24},{2... | collective-permute-start | bytes 1572872 | tf_op jit(solution)/shard_map/ppermute | solution.py:30
  21.3 1.4 %collective-permute-done.3.across = f32[32,8192]{1,0:T(8,128)S(1)} collective-permute-done((f32[32,8192]{1,0:T(8,128)S(1)}, f32[32,8192]{1,0:T(8,128)S(1)}, u32[]{:S(2)}, u32[]{:S(2)}) %collective-permute-start.3) | collective-permute-done | bytes 1048608 | tf_op jit(solution)/shard_map/ppermute | solution.py:36
  22.7 0.3 shard_map.52
  23.0 1.3 %collective-permute-start.5 = (bf16[32,8192]{1,0:T(8,128)(2,1)S(1)}, bf16[32,8192]{1,0:T(8,128)(2,1)S(1)}, u32[]{:S(2)}, u32[]{:S(2)}) collective-permute-start(bf16[32,8192]{1,0:T(8,128)(2,1)S(1)} %shard_map.52), channel_id=1, source_target_pairs={{5,1},{9,5},{13,9},{7,3},{11,7},{15,11},{21,17},{25,21},{29,25},{2... | collective-permute-start | bytes 1572872 | tf_op jit(solution)/shard_map/ppermute | solution.py:30
  24.3 2.6 %shard_map.50.mine = f32[32,8192]{1,0:T(8,128)S(1)} custom-call(f32[386,16,128]{2,1,0:T(8,128)S(1)} %get-tuple-element.17.total, f32[32,8192]{1,0:T(8,128)S(1)} %collective-permute-done.3.across, bf16[32,128,256]{2,1,0:T(8,128)(2,1)S(1)} %get-tuple-element.19.residuals, bf16[128,64,64]{2,1,0:T(8,128)(2,1)S(1)} %get-tuple-element.20.own_map), custom_call_target="tpu_custom_call" | custom-call | bytes 1024 | tf_op jit(solution)/shard_map/pallas_call | solution.py:285
  26.8 0.0 collective-permute-done.4.even
  26.9 10.2 %collective-permute-done.5.odd = bf16[32,8192]{1,0:T(8,128)(2,1)S(1)} collective-permute-done((bf16[32,8192]{1,0:T(8,128)(2,1)S(1)}, bf16[32,8192]{1,0:T(8,128)(2,1)S(1)}, u32[]{:S(2)}, u32[]{:S(2)}) %collective-permute-start.5) | collective-permute-done | bytes 524320 | tf_op jit(solution)/shard_map/ppermute | solution.py:30
  37.1 1.0 %shard_map.53 = f32[32,8192]{1,0:T(8,128)} custom-call(f32[32,8192]{1,0:T(8,128)S(1)} %shard_map.50.mine, bf16[32,8192]{1,0:T(8,128)(2,1)S(1)} %collective-permute-done.4.even, bf16[32,8192]{1,0:T(8,128)(2,1)S(1)} %collective-permute-done.5.odd), custom_call_target="tpu_custom_call" | custom-call | tf_op jit(solution)/shard_map/pallas_call | solution.py:285
  (1 shorter events, 0.0 us)
Async XLA Ops:
  0.0 13.3 %collective-permute-start = (bf16[32,8192]{1,0:T(8,128)(2,1)}, bf16[32,8192]{1,0:T(8,128)(2,1)S(1)}, u32[]{:S(2)}, u32[]{:S(2)}) collective-permute-start(bf16[32,8192]{1,0:T(8,128)(2,1)} %own.1), channel_id=1, source_target_pairs={{1,5},{5,9},{9,13},{3,7},{7,11},{11,15},{17,21},{21,25},{25,29},{1... | collective-permute-start | bytes 1572872 | tf_op jit(solution)/shard_map/ppermute | solution.py:23
  5.1 8.9 %collective-permute-start.2 = (bf16[32,8192]{1,0:T(8,128)(2,1)S(1)}, bf16[32,8192]{1,0:T(8,128)(2,1)S(1)}, u32[]{:S(2)}, u32[]{:S(2)}) collective-permute-start(bf16[32,8192]{1,0:T(8,128)(2,1)S(1)} %shard_map.46.own), channel_id=1, source_target_pairs={{0,4},{4,8},{8,12},{2,6},{6,10},{10,14},{16,20},{20,24},{24,28},{1... | collective-permute-start | bytes 1572872 | tf_op jit(solution)/shard_map/ppermute | solution.py:23
  11.4 3.9 %copy-start = (s32[128,4]{0,1:T(4,128)S(1)}, s32[128,4]{0,1:T(4,128)}, u32[]{:S(2)}) copy-start(s32[128,4]{0,1:T(4,128)} %param.6) | copy-start | bytes 6148
  13.4 2.0 %collective-permute-start.1 = (bf16[32,8192]{1,0:T(8,128)(2,1)S(1)}, bf16[32,8192]{1,0:T(8,128)(2,1)S(1)}, u32[]{:S(2)}, u32[]{:S(2)}) collective-permute-start(bf16[32,8192]{1,0:T(8,128)(2,1)S(1)} %shard_map.48), channel_id=1, source_target_pairs={{0,1},{1,0},{2,3},{3,2},{4,5},{5,4},{6,7},{7,6},{8,9},{9,8},{10,11... | collective-permute-start | bytes 1572872 | tf_op jit(solution)/shard_map/ppermute | solution.py:36
  19.3 3.4 %collective-permute-start.3 = (f32[32,8192]{1,0:T(8,128)S(1)}, f32[32,8192]{1,0:T(8,128)S(1)}, u32[]{:S(2)}, u32[]{:S(2)}) collective-permute-start(f32[32,8192]{1,0:T(8,128)S(1)} %get-tuple-element.18), channel_id=1, source_target_pairs={{0,1},{1,0},{2,3},{3,2},{4,5},{5,4},{6,7},{7,6},{8,9},{9,8},{10,11... | collective-permute-start | bytes 3145736 | tf_op jit(solution)/shard_map/ppermute | solution.py:36
  20.6 6.3 %collective-permute-start.4 = (bf16[32,8192]{1,0:T(8,128)(2,1)S(1)}, bf16[32,8192]{1,0:T(8,128)(2,1)S(1)}, u32[]{:S(2)}, u32[]{:S(2)}) collective-permute-start(bf16[32,8192]{1,0:T(8,128)(2,1)S(1)} %shard_map.51), channel_id=1, source_target_pairs={{4,0},{8,4},{12,8},{6,2},{10,6},{14,10},{20,16},{24,20},{28,24},{2... | collective-permute-start | bytes 1572872 | tf_op jit(solution)/shard_map/ppermute | solution.py:30
  23.0 14.1 %collective-permute-start.5 = (bf16[32,8192]{1,0:T(8,128)(2,1)S(1)}, bf16[32,8192]{1,0:T(8,128)(2,1)S(1)}, u32[]{:S(2)}, u32[]{:S(2)}) collective-permute-start(bf16[32,8192]{1,0:T(8,128)(2,1)S(1)} %shard_map.52), channel_id=1, source_target_pairs={{5,1},{9,5},{13,9},{7,3},{11,7},{15,11},{21,17},{25,21},{29,25},{2... | collective-permute-start | bytes 1572872 | tf_op jit(solution)/shard_map/ppermute | solution.py:30

commit v6 on v5

--- a/solution.py
+++ b/solution.py
@@ -136,8 +136,8 @@
 
 
 def main_kernel(
-    cond, live, one, two_even, two_odd, window_in, total_in, near_map, own_part,
-    out_one, window, total, residuals, index,
+    cond_in, live, one, two_even, two_odd, window_in, total_in, near_map, own_part,
+    out_one, window, total, residuals, index, cond, sem,
 ):
     chains = window.shape[1]
     half = chains // 2
@@ -145,6 +145,8 @@
 
     core = lax.axis_index("rep")
     base = (lax.axis_index("curve") * 2 + core - 2) * blocks
+    fetch = pltpu.make_async_copy(cond_in, cond, sem)
+    fetch.start()
     spread(one, window, blocks)
 
     @pl.when(core == 0)
@@ -207,6 +209,7 @@
             for k, term in enumerate((t0, t1, t2, t3)):
                 total[at[k]] = old[k] + term
 
+    fetch.wait()
     groups = blocks // GROUP
     for q in range(groups + LAG):
         if q < groups:
@@ -354,11 +357,13 @@
     to_one, _, total, residuals = call(
         main_kernel,
         (wide, window_shape, total_shape, jax.ShapeDtypeStruct(group_shape, jnp.bfloat16)),
-        [SMEM] * 2 + [VMEM] * 7,
-        (jnp.transpose(cond), live, one, two_even, two_odd, window, total, near_map, own_part),
+        [HBM, SMEM] + [VMEM] * 7,
+        (in_hbm(jnp.transpose(cond)), live, one, two_even, two_odd, window, total, near_map, own_part),
         out_specs=(VMEM,) * 4,
         scratch_shapes=[
             pltpu.SMEM((blocks * KN,), jnp.int32),
+            pltpu.SMEM((KN, blocks), jnp.int32),
+            pltpu.SemaphoreType.DMA,
         ],
         input_output_aliases={5: 1, 6: 2},
         compiler_params=params(12),
@@ -397,7 +402,7 @@
         out_specs=HBM,
         scratch_shapes=[
             pltpu.VMEM((chains, row_count), jnp.float32),
-            pltpu.SemaphoreType.DMA((PIECES,)),
+            pltpu.SemaphoreType.DMA((2 * PIECES,)),
         ],
         compiler_params=params(8),
     )

time: 38.3 us -> 37.9 us (0.990)
  Pallas kernels: 14.7 us -> 14.1 us
    pallas_call x8, Pallas kernels: 14.7 us -> 14.1 us  [call(): pl.pallas_call(kernel, out_shape=outs, in_specs=specs, out_specs=out_spec...]
  transfers between devices with their start and end apart: 6 -> 6, of which waited for: 4 -> 4; matrix products, arithmetic and copies ran while one was open for 0% -> 0% of each run, Pallas kernels for 25% -> 26%
where the time goes in v6:
time: 37.9 us; the launch traced here: 37.6 us
  waiting for transfers between devices  14.9 us (39%)
  Pallas kernels  14.1 us (37%)
  starting transfers between devices  7.88 us (21%)
  between operations  0.76 us (2%)
    pallas_call x8, Pallas kernels, call(): pl.pallas_call(kernel, out_shape=outs, in_specs=specs, out_specs=out_spec...  14.1 us
    ppermute x2, waiting for transfers between devices, from_next_chip(): lax.ppermute(block, ('curve', 'rep'), [(2 * z + 2 + core, 2 * z + core) f...  10.3 us
    ppermute x2, starting transfers between devices, to_next_chip(): lax.ppermute(block, ('curve', 'rep'), [(2 * z + core, 2 * z + 2 + core) f...  4.74 us
    ppermute x2, waiting for transfers between devices, swap(): return lax.ppermute(block, 'rep', [(0, 1), (1, 0)])  2.66 us
    ppermute x2, starting transfers between devices, from_next_chip(): lax.ppermute(block, ('curve', 'rep'), [(2 * z + 2 + core, 2 * z + core) f...  1.99 us
    ppermute x2, waiting for transfers between devices, to_next_chip(): lax.ppermute(block, ('curve', 'rep'), [(2 * z + core, 2 * z + 2 + core) f...  1.87 us
    ppermute x2, starting transfers between devices, swap(): return lax.ppermute(block, 'rep', [(0, 1), (1, 0)])  1.15 us
  transfers between devices with their start and end apart: 6, of which 4 were waited for; matrix products, arithmetic and copies ran while one was open for 0% of the time, Pallas kernels for 26%

profile of v6, /device:TPU:1, one launch (start us, length us, event | category | flops | bytes accessed | tf_op | source)
XLA Modules:
  0.0 37.6 jit_solution(14286332675656786833)
XLA Ops:
  0.0 4.0 %collective-permute-start = (bf16[32,8192]{1,0:T(8,128)(2,1)}, bf16[32,8192]{1,0:T(8,128)(2,1)S(1)}, u32[]{:S(2)}, u32[]{:S(2)}) collective-permute-start(bf16[32,8192]{1,0:T(8,128)(2,1)} %own.1), channel_id=1, source_target_pairs={{1,5},{5,9},{9,13},{3,7},{7,11},{11,15},{17,21},{21,25},{25,29},{1... | collective-permute-start | bytes 1572872 | tf_op jit(solution)/shard_map/ppermute | solution.py:23
  4.1 1.1 %shard_map.46.own = bf16[32,8192]{1,0:T(8,128)(2,1)S(1)} custom-call(bf16[32,8192]{1,0:T(8,128)(2,1)} %own.1), custom_call_target="tpu_custom_call" | custom-call | bytes 1024 | tf_op jit(solution)/shard_map/pallas_call | solution.py:288
  5.1 0.7 %collective-permute-start.2 = (bf16[32,8192]{1,0:T(8,128)(2,1)S(1)}, bf16[32,8192]{1,0:T(8,128)(2,1)S(1)}, u32[]{:S(2)}, u32[]{:S(2)}) collective-permute-start(bf16[32,8192]{1,0:T(8,128)(2,1)S(1)} %shard_map.46.own), channel_id=1, source_target_pairs={{0,4},{4,8},{8,12},{2,6},{6,10},{10,14},{16,20},{20,24},{24,28},{1... | collective-permute-start | bytes 1572872 | tf_op jit(solution)/shard_map/ppermute | solution.py:23
  5.8 5.6 %shard_map.47 = (bf16[386,32,128]{2,1,0:T(8,128)(2,1)S(1)}, f32[386,16,128]{2,1,0:T(8,128)S(1)}, bf16[128,64,64]{2,1,0:T(8,128)(2,1)S(1)}, bf16[128,64,256]{2,1,0:T(8,128)(2,1)S(1)}, f32[32,128,256]{2,1,0:T(8,128)S(1)}) custom-call(bf16[32,8192]{1,0:T(8,128)(2,1)S(1)} %shard_map.46.own, bf16[64,320,128]{2,1,0:T(8,128)(2,1)} %bitcast.2), custom_call_target="tpu_custom_call" | custom-call | bytes 14680064 | tf_op jit(solution)/shard_map/pallas_call | solution.py:288
  11.4 1.9 %collective-permute-done.arrived.two_odd = bf16[32,8192]{1,0:T(8,128)(2,1)S(1)} collective-permute-done((bf16[32,8192]{1,0:T(8,128)(2,1)}, bf16[32,8192]{1,0:T(8,128)(2,1)S(1)}, u32[]{:S(2)}, u32[]{:S(2)}) %collective-permute-start) | collective-permute-done | bytes 524320 | tf_op jit(solution)/shard_map/ppermute | solution.py:23
  13.4 0.1 collective-permute-start.1
  14.1 0.0 collective-permute-done.2.two_even
  14.1 1.2 %collective-permute-done.1.one = bf16[32,8192]{1,0:T(8,128)(2,1)S(1)} collective-permute-done((bf16[32,8192]{1,0:T(8,128)(2,1)S(1)}, bf16[32,8192]{1,0:T(8,128)(2,1)S(1)}, u32[]{:S(2)}, u32[]{:S(2)}) %collective-permute-start.1) | collective-permute-done | bytes 524320 | tf_op jit(solution)/shard_map/ppermute | solution.py:36
  15.3 3.5 %shard_map.49 = (f32[32,8192]{1,0:T(8,128)S(1)}, bf16[386,32,128]{2,1,0:T(8,128)(2,1)S(1)}, f32[386,16,128]{2,1,0:T(8,128)S(1)}, bf16[32,128,256]{2,1,0:T(8,128)(2,1)S(1)}) custom-call(s32[4,128]{1,0:T(4,128)} %bitcast.3, s32[1]{0:T(128)S(6)} %copy.9.live, ...), custom_call_target="tpu_custom_call", output_to_operand_aliasing={{1}: (5, {}), {2}: (6, {})} | custom-call | flops 1342177280 | bytes 8388608 | tf_op jit(solution)/shard_map/pallas_call | solution.py:288
  18.8 1.1 %collective-permute-start.3 = (f32[32,8192]{1,0:T(8,128)S(1)}, f32[32,8192]{1,0:T(8,128)S(1)}, u32[]{:S(2)}, u32[]{:S(2)}) collective-permute-start(f32[32,8192]{1,0:T(8,128)S(1)} %get-tuple-element.18), channel_id=1, source_target_pairs={{0,1},{1,0},{2,3},{3,2},{4,5},{5,4},{6,7},{7,6},{8,9},{9,8},{10,11... | collective-permute-start | bytes 3145736 | tf_op jit(solution)/shard_map/ppermute | solution.py:36
  19.9 0.2 shard_map.51
  20.1 0.7 %collective-permute-start.4 = (bf16[32,8192]{1,0:T(8,128)(2,1)S(1)}, bf16[32,8192]{1,0:T(8,128)(2,1)S(1)}, u32[]{:S(2)}, u32[]{:S(2)}) collective-permute-start(bf16[32,8192]{1,0:T(8,128)(2,1)S(1)} %shard_map.51), channel_id=1, source_target_pairs={{4,0},{8,4},{12,8},{6,2},{10,6},{14,10},{20,16},{24,20},{28,24},{2... | collective-permute-start | bytes 1572872 | tf_op jit(solution)/shard_map/ppermute | solution.py:30
  20.8 1.4 %collective-permute-done.3.across = f32[32,8192]{1,0:T(8,128)S(1)} collective-permute-done((f32[32,8192]{1,0:T(8,128)S(1)}, f32[32,8192]{1,0:T(8,128)S(1)}, u32[]{:S(2)}, u32[]{:S(2)}) %collective-permute-start.3) | collective-permute-done | bytes 1048608 | tf_op jit(solution)/shard_map/ppermute | solution.py:36
  22.2 0.2 shard_map.52
  22.4 1.3 %collective-permute-start.5 = (bf16[32,8192]{1,0:T(8,128)(2,1)S(1)}, bf16[32,8192]{1,0:T(8,128)(2,1)S(1)}, u32[]{:S(2)}, u32[]{:S(2)}) collective-permute-start(bf16[32,8192]{1,0:T(8,128)(2,1)S(1)} %shard_map.52), channel_id=1, source_target_pairs={{5,1},{9,5},{13,9},{7,3},{11,7},{15,11},{21,17},{25,21},{29,25},{2... | collective-permute-start | bytes 1572872 | tf_op jit(solution)/shard_map/ppermute | solution.py:30
  23.7 2.5 %shard_map.50.mine = f32[32,8192]{1,0:T(8,128)S(1)} custom-call(f32[386,16,128]{2,1,0:T(8,128)S(1)} %get-tuple-element.17.total, f32[32,8192]{1,0:T(8,128)S(1)} %collective-permute-done.3.across, bf16[32,128,256]{2,1,0:T(8,128)(2,1)S(1)} %get-tuple-element.19.residuals, bf16[128,64,64]{2,1,0:T(8,128)(2,1)S(1)} %get-tuple-element.20.own_map), custom_call_target="tpu_custom_call" | custom-call | bytes 1024 | tf_op jit(solution)/shard_map/pallas_call | solution.py:288
  26.3 0.0 collective-permute-done.4.even
  26.3 10.3 %collective-permute-done.5.odd = bf16[32,8192]{1,0:T(8,128)(2,1)S(1)} collective-permute-done((bf16[32,8192]{1,0:T(8,128)(2,1)S(1)}, bf16[32,8192]{1,0:T(8,128)(2,1)S(1)}, u32[]{:S(2)}, u32[]{:S(2)}) %collective-permute-start.5) | collective-permute-done | bytes 524320 | tf_op jit(solution)/shard_map/ppermute | solution.py:30
  36.6 1.0 %shard_map.53 = f32[32,8192]{1,0:T(8,128)} custom-call(f32[32,8192]{1,0:T(8,128)S(1)} %shard_map.50.mine, bf16[32,8192]{1,0:T(8,128)(2,1)S(1)} %collective-permute-done.4.even, bf16[32,8192]{1,0:T(8,128)(2,1)S(1)} %collective-permute-done.5.odd), custom_call_target="tpu_custom_call" | custom-call | tf_op jit(solution)/shard_map/pallas_call | solution.py:288
  (1 shorter events, 0.0 us)
Async XLA Ops:
  0.0 13.3 %collective-permute-start = (bf16[32,8192]{1,0:T(8,128)(2,1)}, bf16[32,8192]{1,0:T(8,128)(2,1)S(1)}, u32[]{:S(2)}, u32[]{:S(2)}) collective-permute-start(bf16[32,8192]{1,0:T(8,128)(2,1)} %own.1), channel_id=1, source_target_pairs={{1,5},{5,9},{9,13},{3,7},{7,11},{11,15},{17,21},{21,25},{25,29},{1... | collective-permute-start | bytes 1572872 | tf_op jit(solution)/shard_map/ppermute | solution.py:23
  5.1 8.9 %collective-permute-start.2 = (bf16[32,8192]{1,0:T(8,128)(2,1)S(1)}, bf16[32,8192]{1,0:T(8,128)(2,1)S(1)}, u32[]{:S(2)}, u32[]{:S(2)}) collective-permute-start(bf16[32,8192]{1,0:T(8,128)(2,1)S(1)} %shard_map.46.own), channel_id=1, source_target_pairs={{0,4},{4,8},{8,12},{2,6},{6,10},{10,14},{16,20},{20,24},{24,28},{1... | collective-permute-start | bytes 1572872 | tf_op jit(solution)/shard_map/ppermute | solution.py:23
  13.4 2.0 %collective-permute-start.1 = (bf16[32,8192]{1,0:T(8,128)(2,1)S(1)}, bf16[32,8192]{1,0:T(8,128)(2,1)S(1)}, u32[]{:S(2)}, u32[]{:S(2)}) collective-permute-start(bf16[32,8192]{1,0:T(8,128)(2,1)S(1)} %shard_map.48), channel_id=1, source_target_pairs={{0,1},{1,0},{2,3},{3,2},{4,5},{5,4},{6,7},{7,6},{8,9},{9,8},{10,11... | collective-permute-start | bytes 1572872 | tf_op jit(solution)/shard_map/ppermute | solution.py:36
  18.8 3.4 %collective-permute-start.3 = (f32[32,8192]{1,0:T(8,128)S(1)}, f32[32,8192]{1,0:T(8,128)S(1)}, u32[]{:S(2)}, u32[]{:S(2)}) collective-permute-start(f32[32,8192]{1,0:T(8,128)S(1)} %get-tuple-element.18), channel_id=1, source_target_pairs={{0,1},{1,0},{2,3},{3,2},{4,5},{5,4},{6,7},{7,6},{8,9},{9,8},{10,11... | collective-permute-start | bytes 3145736 | tf_op jit(solution)/shard_map/ppermute | solution.py:36
  20.1 6.2 %collective-permute-start.4 = (bf16[32,8192]{1,0:T(8,128)(2,1)S(1)}, bf16[32,8192]{1,0:T(8,128)(2,1)S(1)}, u32[]{:S(2)}, u32[]{:S(2)}) collective-permute-start(bf16[32,8192]{1,0:T(8,128)(2,1)S(1)} %shard_map.51), channel_id=1, source_target_pairs={{4,0},{8,4},{12,8},{6,2},{10,6},{14,10},{20,16},{24,20},{28,24},{2... | collective-permute-start | bytes 1572872 | tf_op jit(solution)/shard_map/ppermute | solution.py:30
  22.4 14.2 %collective-permute-start.5 = (bf16[32,8192]{1,0:T(8,128)(2,1)S(1)}, bf16[32,8192]{1,0:T(8,128)(2,1)S(1)}, u32[]{:S(2)}, u32[]{:S(2)}) collective-permute-start(bf16[32,8192]{1,0:T(8,128)(2,1)S(1)} %shard_map.52), channel_id=1, source_target_pairs={{5,1},{9,5},{13,9},{7,3},{11,7},{15,11},{21,17},{25,21},{29,25},{2... | collective-permute-start | bytes 1572872 | tf_op jit(solution)/shard_map/ppermute | solution.py:30
